TPU v7x, 32 devices: a whole 2x2x4 slice. The times are simulated.
32 devices in a mesh: dp: 16 (over z, y, x), mp: 2 (over core).
Axes of the slice: x: 2, y: 2, z: 4, core: 2. Of those that a mesh axis runs over, the one named last changes fastest.
Arguments:
- inputs: bfloat16 [32768, 1024], P('dp', 'mp'), may hold values from -6 to 6
- lengths: int32 [64], P('dp'), may hold values from 80 to 512, as said below
- w_query: bfloat16 [1024, 1024], P(None, 'mp'), may hold values from -0.1875 to 0.1875
- b_query: bfloat16 [1024], P('mp'), may hold values from -3 to 3
- w_key: bfloat16 [1024, 1024], P(None, 'mp'), may hold values from -0.1875 to 0.1875
- w_value: bfloat16 [1024, 1024], P(None, 'mp'), may hold values from -0.1875 to 0.1875
- b_value: bfloat16 [1024], P('mp'), may hold values from -3 to 3
- w_out: bfloat16 [1024, 1024], P('mp'), may hold values from -1.5 to 1.5
- b_out: bfloat16 [1024], P('mp'), may hold values from -3 to 3
- gain_one: bfloat16 [1024], P('mp'), may hold values from 0.5 to 1.5
- shift_one: bfloat16 [1024], P('mp'), may hold values from -3 to 3
- w_in: bfloat16 [1024, 4096], P(None, 'mp'), may hold values from -0.1875 to 0.1875
- b_in: bfloat16 [4096], P('mp'), may hold values from -3 to 3
- w_back: bfloat16 [4096, 1024], P('mp'), may hold values from -0.09375 to 0.09375
- b_back: bfloat16 [1024], P('mp'), may hold values from -3 to 3
- gain_two: bfloat16 [1024], P('mp'), may hold values from 0.5 to 1.5
- shift_two: bfloat16 [1024], P('mp'), may hold values from -3 to 3
- cotangent: bfloat16 [32768, 1024], P('dp', 'mp'), may hold values from -6 to 6
Outputs:
- output: bfloat16 [32768, 1024], P('dp', 'mp')
- input_grad: bfloat16 [32768, 1024], P('dp', 'mp')
- grad_w_query: float32 [1024, 1024], P(None, 'mp')
- grad_b_query: float32 [1024], P('mp')
- grad_w_key: float32 [1024, 1024], P(None, 'mp')
- grad_w_value: float32 [1024, 1024], P(None, 'mp')
- grad_b_value: float32 [1024], P('mp')
- grad_w_out: float32 [1024, 1024], P('mp')
- grad_b_out: float32 [1024], P('mp')
- grad_gain_one: float32 [1024], P('mp')
- grad_shift_one: float32 [1024], P('mp')
- grad_w_in: float32 [1024, 4096], P(None, 'mp')
- grad_b_in: float32 [4096], P('mp')
- grad_w_back: float32 [4096, 1024], P('mp')
- grad_b_back: float32 [1024], P('mp')
- grad_gain_two: float32 [1024], P('mp')
- grad_shift_two: float32 [1024], P('mp')
Inputs may be any that keep to these rules, and one draw needn't show every extreme that they name: `lengths`: real tokens of each page; some page has exactly 512 and some exactly 80.
All inputs are finite; a program needn't handle non-finite values.
Results may differ from a plain program's by a relative error of at most 0.02.
Values may be sent and summed in bfloat16 or wider, within the bound.
A program may use at most 192 MiB of HBM per device.

v0:
```python
import functools

import jax
import jax.numpy as jnp
from jax import lax
from jax.experimental import pallas as pl
from jax.experimental.pallas import tpu as pltpu
from jax.sharding import PartitionSpec as P

MESH = pl.DeviceIdType.MESH
HDIM = 64
eps = 1e-05
LOG2_E = 1.4426950408889634
CDF_TERMS = (
    7.97884941e-01, 3.63330844e-02, -3.25946972e-05, -5.53063392e-05, 3.96477773e-06, -1.32266680e-07, 1.75628964e-09,
)


QUARTER = 16
CHUNK = 4 * QUARTER
PAIR = 2 * CHUNK
BLOCK = 4 * PAIR
SLOTS = 16
STAGES = (0, 2, 4, 6, 8, 10, 12, 14)


def rows_at(start, size):
    return pl.ds(pl.multiple_of(start, QUARTER), size)


def chip_sum(pairs, grads, out, land_a, land_z, land_m, land_b, ssem, rsem, osem):
    dp = lax.axis_index("dp")
    mp = lax.axis_index("mp")
    z, y, x = dp // 4, (dp // 2) % 2, dp % 2
    inner = (z == 1) | (z == 2)
    outer = jnp.logical_not(inner)
    quarter = jnp.where(z == 1, 0, 1)

    def chip(cz, cy, cx):
        return (cz * 4 + cy * 2 + cx, mp)

    first_peer = (chip(z, y, 1 - x), chip(z, 1 - y, x))
    second_peer = (chip(z, 1 - y, x), chip(z, y, 1 - x))
    side = (x, y)
    inward = chip(jnp.where(z == 0, 1, 2), y, x)
    outward = chip(jnp.where(z == 1, 0, 3), y, x)
    across = chip(3 - z, y, x)
    twin = (dp, 1 - mp)

    def meet():
        barrier = pltpu.get_barrier_semaphore()
        for peer in first_peer + (twin,):
            pl.semaphore_signal(barrier, 1, device_id=peer, device_id_type=MESH)

        @pl.when(inner)
        def _():
            for peer in (outward, across):
                pl.semaphore_signal(barrier, 1, device_id=peer, device_id_type=MESH)
            pl.semaphore_wait(barrier, 5)

        @pl.when(outer)
        def _():
            pl.semaphore_signal(barrier, 1, device_id=inward, device_id_type=MESH)
            pl.semaphore_wait(barrier, 4)

    def half(ref, kind, k, which):
        return ref.at[rows_at(k * PAIR + kind * CHUNK + which * 2 * QUARTER, 2 * QUARTER)]

    def own(kind, k):
        return half(grads, kind, k, side[kind])

    def own_out(kind, k):
        return half(out, kind, k, side[kind])

    def part_of(ref, kind, k, which):
        return ref.at[rows_at(k * PAIR + kind * CHUNK + (side[kind] * 2 + which) * QUARTER, QUARTER)]

    def part(kind, k, which):
        return part_of(grads, kind, k, which)

    def keep(kind, k):
        return pltpu.make_async_copy(
            part(kind, k, quarter), part_of(out, kind, k, quarter), osem.at[kind, lax.rem(k, SLOTS)]
        )

    def send(stage, kind, k, source, target, peer):
        slot = lax.rem(k, SLOTS)
        return pltpu.make_async_remote_copy(
            source,
            target,
            ssem.at[stage, kind, slot],
            rsem.at[stage, kind, slot],
            device_id=peer,
            device_id_type=MESH,
        )

    def landing(buffer, kind, k):
        return buffer.at[lax.rem(k, SLOTS), kind]

    def scatter_first(kind, k):
        return send(0, kind, k, half(grads, kind, k, 1 - side[kind]), landing(land_a, kind, k), first_peer[kind])

    def go_in(kind, k):
        return send(1, kind, k, own(kind, k), landing(land_z, kind, k), inward)

    def scatter_across(kind, k):
        return send(2, kind, k, part(kind, k, 1 - quarter), landing(land_m, kind, k), across)

    def swap_second(kind, k):
        return send(3, kind, k, part(kind, k, quarter), landing(land_b, kind, k), second_peer[kind])

    def gather_across(kind, k):
        return send(4, kind, k, part(kind, k, quarter), part_of(out, kind, k, quarter), across)

    def go_out(kind, k):
        return send(5, kind, k, own_out(kind, k), own_out(kind, k), outward)

    def gather_first(kind, k):
        return send(6, kind, k, own_out(kind, k), own_out(kind, k), first_peer[kind])

    def step(t):
        ks = [t - offset for offset in STAGES]
        live = [(k >= 0) & (k < pairs) for k in ks]

        @pl.when(live[7])
        def _():
            for kind in (0, 1):
                gather_first(kind, ks[7]).wait()

        @pl.when(live[6] & inner)
        def _():
            for kind in (0, 1):
                go_out(kind, ks[6]).wait_send()

        @pl.when(live[6] & outer)
        def _():
            for kind in (0, 1):
                go_out(kind, ks[6]).wait_recv()
                gather_first(kind, ks[6]).start()

        @pl.when(live[5] & inner)
        def _():
            for kind in (0, 1):
                gather_across(kind, ks[5]).wait()
                keep(kind, ks[5]).wait()
                go_out(kind, ks[5]).start()
                gather_first(kind, ks[5]).start()

        @pl.when(live[4] & inner)
        def _():
            for kind in (0, 1):
                swap_second(kind, ks[4]).wait()
                add_into(part(kind, ks[4], quarter), landing(land_b, kind, ks[4]))
                gather_across(kind, ks[4]).start()
                keep(kind, ks[4]).start()

        @pl.when(live[3] & inner)
        def _():
            for kind in (0, 1):
                scatter_across(kind, ks[3]).wait()
                add_into(part(kind, ks[3], quarter), landing(land_m, kind, ks[3]))
                swap_second(kind, ks[3]).start()

        @pl.when(live[2] & inner)
        def _():
            for kind in (0, 1):
                go_in(kind, ks[2]).wait_recv()
                add_into(own(kind, ks[2]), landing(land_z, kind, ks[2]))
                scatter_across(kind, ks[2]).start()

        @pl.when(live[2] & outer)
        def _():
            for kind in (0, 1):
                go_in(kind, ks[2]).wait_send()

        @pl.when(live[1])
        def _():
            for kind in (0, 1):
                scatter_first(kind, ks[1]).wait()
                add_into(own(kind, ks[1]), landing(land_a, kind, ks[1]))

                @pl.when(outer)
                def _():
                    go_in(kind, ks[1]).start()

        @pl.when(live[0])
        def _():
            for kind in (0, 1):
                scatter_first(kind, ks[0]).start()

    return meet, step


def add_into(target, arrived):
    total = target[...].astype(jnp.float32) + arrived[...].astype(jnp.float32)
    target[...] = total.astype(jnp.bfloat16)


def dot_tn(left, right):
    return lax.dot_general(left, right, (((0,), (0,)), ((), ())), preferred_element_type=jnp.float32)


def dot_nt(left, right):
    return lax.dot_general(left, right, (((1,), (1,)), ((), ())), preferred_element_type=jnp.float32)


def gelu_and_slope(v):
    square = v * v
    q = CDF_TERMS[-1] * square + CDF_TERMS[-2]
    for term in CDF_TERMS[-3::-1]:
        q = q * square + term
    cdf = 0.5 * jnp.tanh(v * q) + 0.5
    pdf = jnp.exp2(square * (-0.5 * LOG2_E)) * 0.3989422804014327
    return v * cdf, cdf + v * pdf


def lane_of(rows):
    return lax.broadcasted_iota(jnp.int32, (rows, 128), 1)


def key_lanes(length, rows):
    lane = lane_of(rows) % 64
    slot = lax.broadcasted_iota(jnp.int32, (rows, 128), 0)
    bias = jnp.where(slot < length, 0.0, -1e30)
    return jnp.where(lane < 3, 1.0, jnp.where(lane == 3, bias, 0.0)).astype(jnp.bfloat16)


def layer_kernel(
    inputs, cotangent, w_q, w_k, w_v, w_o, w_in, w_back,
    b_q, b_v, b_in, b_o, g_one, s_one, b_back, g_two, s_two, lens,
    out, out_own, out_recv, ig_own, ig_recv, act_hbm, slope_hbm, w_other, w_oo, w_ino, w_backo,
    grads, land_a, land_z, land_m, land_b, send_t, land_t, send_v, land_v, acc, buf_a, low, buf_c, buf_d, buf_e,
    buf_f, inner_g, qkv, xb, ctx, aux, normed_b, inv_b, vec_own, vec_oth, nat, bias_qkv, bias_ff, bias_in, sums_b, kl,
    ssem, rsem, osem, tsem, trsem, vsem, vrsem, isem, psem, lsem, gsem, xsem, xrsem, fsem, frsem,
):
    dp = lax.axis_index("dp")
    mp = lax.axis_index("mp")
    tokens, full = buf_a.shape
    half = full // 2
    tiles = act_hbm.shape[0]
    wide = act_hbm.shape[2]
    part = wide // 2
    seq = kl.shape[0]
    pages = tokens // seq
    pairs = grads.shape[0] // PAIR
    last_rows = (pairs - 1) * PAIR
    meet, tick = chip_sum(pairs, grads, out, land_a, land_z, land_m, land_b, ssem, rsem, osem)
    own_cols = pl.ds(pl.multiple_of(mp * half, half), half)
    other_cols = pl.ds(pl.multiple_of((1 - mp) * half, half), half)
    own_tokens = pl.ds(pl.multiple_of(mp * tokens, tokens), tokens)
    other_tokens = pl.ds(pl.multiple_of((1 - mp) * tokens, tokens), tokens)
    twin = (dp, 1 - mp)

    def load(i, src, dst):
        return pltpu.make_async_copy(src, dst, lsem.at[i])

    def give(i, src, dst, sends, gets):
        return pltpu.make_async_remote_copy(
            src, dst, sends.at[i], gets.at[i], device_id=twin, device_id_type=MESH
        )

    def weight_rows(n):
        return pl.ds(n * full, full)

    loads = [load(0, inputs.at[own_tokens], xb.at[:, own_cols])]
    loads += [load(1 + n, w, grads.at[weight_rows(n), pl.ds(0, half)]) for n, w in enumerate((w_q, w_k, w_v))]
    loads += [load(4, w_o, buf_f.at[0]), load(5, cotangent.at[own_tokens], buf_a.at[:, own_cols])]
    for copy in loads:
        copy.start()
    vec_own[...] = jnp.zeros_like(vec_own)
    at_row = 0
    for ref in (b_q, b_v, b_in, b_o, g_one, s_one, b_back, g_two, s_two):
        for c in range(0, ref.shape[0], half):
            vec_own[at_row : at_row + 1, :] = ref[c : c + half].astype(jnp.float32).reshape(1, half)
            at_row += 1
    meet()
    gifts = [
        give(0, inputs.at[other_tokens], xb.at[:, own_cols], xsem, xrsem),
        give(1, vec_own, vec_oth, xsem, xrsem),
    ]
    gifts += [
        give(2 + n, w, grads.at[weight_rows(n), pl.ds(half, half)], xsem, xrsem)
        for n, w in enumerate((w_q, w_k, w_v))
    ]
    gifts += [
        give(5, w_o, buf_f.at[1], xsem, xrsem),
        give(6, cotangent.at[other_tokens], buf_a.at[:, own_cols], xsem, xrsem),
    ]
    for gift in gifts:
        gift.start()

    def ff_gifts(j):
        at = pl.ds(pl.multiple_of(j * part, part), part)
        return (
            pltpu.make_async_remote_copy(
                w_in.at[:, at], w_ino.at[:, at], fsem.at[j, 0], frsem.at[j, 0], device_id=twin, device_id_type=MESH
            ),
            pltpu.make_async_remote_copy(
                w_back.at[at], w_backo.at[at], fsem.at[j, 1], frsem.at[j, 1], device_id=twin, device_id_type=MESH
            ),
        )

    gifts[1].wait_recv()
    nat[:, own_cols] = vec_own[...]
    nat[:, other_cols] = vec_oth[...]
    for n, row in enumerate((0, None, 1)):
        for h, ref in enumerate((vec_own, vec_oth)):
            at = slice(h * half, (h + 1) * half)
            if row is None:
                bias_qkv[n : n + 1, at] = jnp.zeros((1, half), jnp.float32)
            else:
                bias_qkv[n : n + 1, at] = ref[row : row + 1, :]
    for j in range(tiles):
        at = slice((j % 2) * part, (j % 2 + 1) * part)
        row = 2 + j // 2
        bias_ff[j : j + 1, :part] = vec_own[row : row + 1, at]
        bias_ff[j : j + 1, part:] = vec_oth[row : row + 1, at]
    loads[0].wait()
    gifts[0].wait_recv()

    for n in range(3):
        loads[1 + n].wait()
        gifts[2 + n].wait_recv()
        if n == 2:
            def start_gifts(j, carry):
                for gift in ff_gifts(j):
                    gift.start()
                return carry

            lax.fori_loop(0, tiles, start_gifts, 0)

        for h in (0, 1):
            at = slice(h * half, (h + 1) * half)
            made = jnp.dot(xb[...], grads[n * full : (n + 1) * full, at], preferred_element_type=jnp.float32)
            qkv[2 * n + h] = (made + bias_qkv[n : n + 1, at]).astype(jnp.bfloat16)

    keeps = [load(6 + n, grads.at[weight_rows(n), pl.ds(half, half)], w_other.at[n]) for n in range(3)]
    for copy in keeps:
        copy.start()
    gifts[5].wait_recv()
    keeps.append(load(9, buf_f.at[1], w_oo))
    keeps[3].start()
    loads[4].wait()

    lane = lane_of(seq)
    low_lanes = lane < 64
    q_one = jnp.where(lane % 64 == 3, 1.0, 0.0).astype(jnp.bfloat16)

    def pair_forward(i, carry):
        page, pair = i // 8, lax.rem(i, 8)

        @pl.when(pair == 0)
        def _():
            kl[...] = key_lanes(lens[mp * pages + page], seq)

        rows = pl.ds(pl.multiple_of(page * seq, seq), seq)
        side = pair // 4
        cols = pl.ds(pl.multiple_of(lax.rem(pair, 4) * 128, 128), 128)
        kp = qkv[2 + side, rows, cols]
        vp = qkv[4 + side, rows, cols]
        qp = qkv[side, rows, cols] * jnp.bfloat16(0.125)
        one = jnp.ones_like(vp)
        outs = []
        for h in (0, 1):
            mine = low_lanes if h == 0 else jnp.logical_not(low_lanes)
            scores = dot_nt(jnp.where(mine, qp, q_one), jnp.where(mine, kp, kl[...]))
            top = jnp.max(scores, axis=1, keepdims=True)
            weights = jnp.exp(scores - top).astype(jnp.bfloat16)
            outs.append((top, jnp.dot(weights, jnp.where(mine, vp, one), preferred_element_type=jnp.float32)))
        (top0, out0), (top1, out1) = outs
        total = jnp.where(low_lanes, out1, out0)
        value = jnp.where(low_lanes, out0, out1) / pltpu.roll(total, 64, 1)
        neg = -(jnp.where(low_lanes, top1, top0) + jnp.log(total))
        first = neg.astype(jnp.bfloat16)
        rest = neg - first.astype(jnp.float32)
        second = rest.astype(jnp.bfloat16)
        third = (rest - second.astype(jnp.float32)).astype(jnp.bfloat16)
        at = lane % 64
        mixed = jnp.where(at == 0, first, jnp.where(at == 1, second, jnp.where(at == 2, third, q_one)))
        ctx[side, rows, cols] = value.astype(jnp.bfloat16)
        aux[side, rows, cols] = mixed
        return carry

    lax.fori_loop(0, 8 * pages, pair_forward, 0)

    def fetch_in(j, slot):
        at = pl.ds(pl.multiple_of(j * part, part), part)
        return [
            pltpu.make_async_copy(w_in.at[:, at], buf_e.at[slot, :, pl.ds(0, part)], isem.at[slot, 2]),
            pltpu.make_async_copy(w_ino.at[:, at], buf_e.at[slot, :, pl.ds(part, part)], isem.at[slot, 3]),
        ]

    def fetch_back(j, slot):
        at = pl.ds(pl.multiple_of(j * part, part), part)
        return [
            pltpu.make_async_copy(w_back.at[at], buf_f.at[slot, pl.ds(0, part)], isem.at[slot, 4]),
            pltpu.make_async_copy(w_backo.at[at], buf_f.at[slot, pl.ds(part, part)], isem.at[slot, 5]),
        ]

    def fetch_made(j, slot):
        return [
            pltpu.make_async_copy(act_hbm.at[j], buf_c.at[slot], isem.at[slot, 0]),
            pltpu.make_async_copy(slope_hbm.at[j], buf_d.at[slot], isem.at[slot, 1]),
        ]

    def start(copies):
        for copy in copies:
            copy.start()

    def finish(copies):
        for copy in copies:
            copy.wait()

    def got_gifts(j):
        for gift in ff_gifts(j):
            gift.wait_recv()

    got_gifts(0)
    start(fetch_in(0, 0))
    step = 256

    def norm_one(i, carry):
        rows = pl.ds(pl.multiple_of(i * step, step), step)
        attended = (
            xb[rows, :].astype(jnp.float32)
            + jnp.dot(ctx[0, rows, :], buf_f[0], preferred_element_type=jnp.float32)
            + jnp.dot(ctx[1, rows, :], buf_f[1], preferred_element_type=jnp.float32)
            + nat[6:7, :]
        )
        average = jnp.mean(attended, axis=1, keepdims=True)
        centred = attended - average
        inv = lax.rsqrt(jnp.mean(centred * centred, axis=1, keepdims=True) + eps)
        normed = centred * inv
        hidden = normed * nat[7:8, :] + nat[8:9, :]
        acc[rows, :] = hidden
        low[rows, :] = hidden.astype(jnp.bfloat16)
        normed_b[rows, :] = normed.astype(jnp.bfloat16)
        inv_b[rows, :] = jnp.broadcast_to(inv, (step, 128))
        return carry

    lax.fori_loop(0, tokens // step, norm_one, 0)
    keeps[3].wait()
    start(fetch_back(0, 0))

    def saves(j, slot):
        return [
            pltpu.make_async_copy(buf_c.at[slot], act_hbm.at[j], psem.at[slot, 0]),
            pltpu.make_async_copy(buf_d.at[slot], slope_hbm.at[j], psem.at[slot, 1]),
        ]

    def forward_tile(j, carry):
        slot = lax.rem(j, 2)

        @pl.when(j + 1 < tiles)
        def _():
            got_gifts(j + 1)
            start(fetch_in(j + 1, 1 - slot) + fetch_back(j + 1, 1 - slot))

        finish(fetch_in(j, slot) + fetch_back(j, slot))

        @pl.when(j >= 2)
        def _():
            finish(saves(j - 2, slot))

        for r in range(0, tokens, half):
            rows = pl.ds(r, half)
            inner = jnp.dot(low[rows, :], buf_e[slot], preferred_element_type=jnp.float32) + bias_ff[pl.ds(j, 1), :]
            value, grad = gelu_and_slope(inner)
            value = value.astype(jnp.bfloat16)
            buf_c[slot, rows, :] = value
            buf_d[slot, rows, :] = grad.astype(jnp.bfloat16)
            acc[rows, :] += jnp.dot(value, buf_f[slot], preferred_element_type=jnp.float32)
        start(saves(j, slot))
        return carry

    lax.fori_loop(0, tiles, forward_tile, 0)
    loads[5].wait()
    gifts[6].wait_recv()
    stage_rows = tiles * BLOCK

    def norm_two(i, sums):
        at = pl.multiple_of(i * step, step)
        rows = pl.ds(at, step)
        summed = acc[rows, :] + nat[9:10, :]
        average = jnp.mean(summed, axis=1, keepdims=True)
        centred = summed - average
        inv = lax.rsqrt(jnp.mean(centred * centred, axis=1, keepdims=True) + eps)
        normed = centred * inv
        grads[pl.ds(pl.multiple_of(stage_rows + i * step, step), step), :] = (
            normed * nat[10:11, :] + nat[11:12, :]
        ).astype(jnp.bfloat16)
        page = (i * step) // seq
        slots = lax.broadcasted_iota(jnp.int32, (step, 1), 0) + lax.rem(i * step, seq)
        valid = jnp.where(slots < lens[mp * pages + page], 1.0, 0.0)
        grad = buf_a[rows, :].astype(jnp.float32) * valid
        scaled = grad * nat[10:11, :]
        mean_one = jnp.mean(scaled, axis=1, keepdims=True)
        mean_two = jnp.mean(scaled * normed, axis=1, keepdims=True)
        back = inv * (scaled - mean_one - normed * mean_two)
        acc[rows, :] = back
        buf_a[rows, :] = back.astype(jnp.bfloat16)
        return (
            sums[0] + jnp.sum(back, axis=0, keepdims=True),
            sums[1] + jnp.sum(grad * normed, axis=0, keepdims=True),
            sums[2] + jnp.sum(grad, axis=0, keepdims=True),
        )

    zero = jnp.zeros((1, full), jnp.float32)
    for n, row in enumerate(lax.fori_loop(0, tokens // step, norm_two, (zero, zero, zero))):
        sums_b[n : n + 1, :] = row
    finish(keeps[:3])
    staged = grads.at[pl.ds(stage_rows, tokens)]
    out_keep = pltpu.make_async_copy(staged.at[:, own_cols], out_own, gsem.at[3])
    out_send = pltpu.make_async_remote_copy(
        staged.at[:, other_cols], out_recv, gsem.at[4], gsem.at[5], device_id=twin, device_id_type=MESH
    )
    out_keep.start()
    out_send.start()
    grads[last_rows : last_rows + PAIR, :] = jnp.zeros((PAIR, full), jnp.bfloat16)

    def to_twin(b):
        slot = lax.rem(b, 2)
        return pltpu.make_async_remote_copy(
            send_t.at[slot], land_t.at[slot], tsem.at[slot], trsem.at[slot], device_id=twin, device_id_type=MESH
        )

    def take_twin(b):
        to_twin(b).wait_recv()
        slot = lax.rem(b, 2)

        def piece(i, carry):
            add_into(grads.at[rows_at(b * BLOCK + i * CHUNK, CHUNK)], land_t.at[slot, rows_at(i * CHUNK, CHUNK)])
            return carry

        lax.fori_loop(0, BLOCK // CHUNK, piece, 0)

    def backward_tile(b, carry):
        j = tiles - 1 - b
        slot = lax.rem(j, 2)
        mate = lax.rem(b, 2)

        @pl.when(b >= 2)
        def _():
            finish(fetch_made(j, slot) + fetch_in(j, slot) + fetch_back(j, slot))
            to_twin(b - 2).wait_send()

        base = b * BLOCK
        for c in range(0, full, half):
            made = dot_tn(buf_c[slot], buf_a[:, c : c + half]).astype(jnp.bfloat16)
            grads[rows_at(base, part), c : c + half] = made[:part]
            send_t[mate, :part, c : c + half] = made[part:]

        @pl.when(b >= 1)
        def _():
            take_twin(b - 1)
            tick(2 * b - 2)

        total = jnp.zeros((1, wide), jnp.float32)
        for r in range(0, tokens, half):
            rows = pl.ds(r, half)
            made = dot_nt(buf_a[rows, :], buf_f[slot]) * buf_d[slot, rows, :].astype(jnp.float32)
            made = made.astype(jnp.bfloat16)
            inner_g[rows, :] = made
            total = total + jnp.sum(made.astype(jnp.float32), axis=0, keepdims=True)
            acc[rows, :] += dot_nt(made, buf_e[slot])
        bias_in[pl.ds(j, 1), :] = total
        for c in range(0, full, part):
            made = dot_tn(low[:, c : c + part], inner_g[...]).astype(jnp.bfloat16)
            grads[rows_at(base + part, part), c : c + part] = made[:, :part]
            send_t[mate, part:, c : c + part] = made[:, part:]

        to_twin(b).start()

        @pl.when(b < 2)
        def _():
            finish(saves(j, slot))

        @pl.when(b < tiles - 2)
        def _():
            start(fetch_made(j - 2, slot) + fetch_in(j - 2, slot) + fetch_back(j - 2, slot))

        @pl.when(b >= 1)
        def _():
            tick(2 * b - 1)

        return carry

    lax.fori_loop(0, tiles, backward_tile, 0)
    t = 2 * tiles - 2

    second = [load(10, w_o, buf_f.at[0]), load(11, w_oo, buf_f.at[1])]
    start(second)

    def norm_back(i, sums):
        rows = pl.ds(pl.multiple_of(i * step, step), step)
        grad = acc[rows, :]
        normed = normed_b[rows, :].astype(jnp.float32)
        scaled = grad * nat[7:8, :]
        mean_one = jnp.mean(scaled, axis=1, keepdims=True)
        mean_two = jnp.mean(scaled * normed, axis=1, keepdims=True)
        back = inv_b[rows, 0:1] * (scaled - mean_one - normed * mean_two)
        acc[rows, :] = back
        buf_a[rows, :] = back.astype(jnp.bfloat16)
        return (
            sums[0] + jnp.sum(back, axis=0, keepdims=True),
            sums[1] + jnp.sum(grad * normed, axis=0, keepdims=True),
            sums[2] + jnp.sum(grad, axis=0, keepdims=True),
        )

    bias_o, gain_one, shift_one = lax.fori_loop(0, tokens // step, norm_back, (zero, zero, zero))
    tick(t)

    b = tiles
    to_twin(b - 2).wait_send()
    out_keep.wait()
    out_send.wait()
    finish(second)
    for h in (0, 1):
        for c in range(0, full, half):
            made = dot_tn(ctx[h], buf_a[:, c : c + half]).astype(jnp.bfloat16)
            if h == 0:
                grads[b * BLOCK : b * BLOCK + half, c : c + half] = made
            else:
                send_t[b % 2, :, c : c + half] = made
    take_twin(b - 1)
    to_twin(b).start()
    tick(t + 1)
    for h in (0, 1):
        for r in range(0, tokens, half):
            buf_e[h, r : r + half, :] = dot_nt(buf_a[r : r + half, :], buf_f[h]).astype(jnp.bfloat16)
    take_twin(b)
    tick(t + 2)
    t = t + 3

    def pair_backward(i, carry):
        page, pair = i // 8, lax.rem(i, 8)

        @pl.when(pair == 0)
        def _():
            kl[...] = key_lanes(lens[mp * pages + page], seq)

        side = pair // 4
        rows = pl.ds(pl.multiple_of(page * seq, seq), seq)
        cols = pl.ds(pl.multiple_of(lax.rem(pair, 4) * 128, 128), 128)
        qp = qkv[side, rows, cols] * jnp.bfloat16(0.125)
        kp = qkv[2 + side, rows, cols]
        vp = qkv[4 + side, rows, cols]
        extra = aux[side, rows, cols]
        gp = buf_e[side, rows, cols]
        cp = ctx[side, rows, cols]
        none = jnp.zeros_like(gp)
        made = []
        for h in (0, 1):
            mine = low_lanes if h == 0 else jnp.logical_not(low_lanes)
            scores = dot_nt(jnp.where(mine, qp, extra), jnp.where(mine, kp, kl[...]))
            probs = jnp.exp(scores)
            gh = jnp.where(mine, gp, none)
            grad_weights = dot_nt(gh, vp)
            delta = jnp.sum(gh.astype(jnp.float32) * cp.astype(jnp.float32), axis=1, keepdims=True)
            grad_scores = (probs * (grad_weights - delta)).astype(jnp.bfloat16)
            grad_v = dot_tn(probs.astype(jnp.bfloat16), gh)
            grad_q = jnp.dot(grad_scores, jnp.where(mine, kp, none), preferred_element_type=jnp.float32)
            grad_k = dot_tn(grad_scores, jnp.where(mine, qp, none))
            made.append((grad_q * 0.125, grad_k, grad_v))
        for n in range(3):
            qkv[2 * n + side, rows, cols] = (made[0][n] + made[1][n]).astype(jnp.bfloat16)
        tick(t + i)
        return carry

    lax.fori_loop(0, 8 * pages, pair_backward, 0)
    t = t + 8 * pages

    third = [load(12, w_q, buf_c.at[0]), load(13, w_k, buf_d.at[0]), load(14, w_v, buf_e.at[0])]
    third += [load(15 + n, w_other.at[n], ref.at[1]) for n, ref in enumerate((buf_c, buf_d, buf_e))]
    start(third)
    b = tiles + 1

    def weights_loop(i, carry):
        at = b + i
        slot = lax.rem(at, 2)
        to_twin(at - 2).wait_send()
        for r in range(0, full, half):
            made = dot_tn(xb[:, r : r + half], qkv[2 * i]).astype(jnp.bfloat16)
            grads[rows_at(at * BLOCK, BLOCK), r : r + half] = made
            made = dot_tn(xb[:, r : r + half], qkv[2 * i + 1]).astype(jnp.bfloat16)
            send_t[slot, :, r : r + half] = made

        @pl.when(i >= 1)
        def _():
            take_twin(at - 1)

        to_twin(at).start()
        tick(t + i)
        return carry

    lax.fori_loop(0, 3, weights_loop, 0)
    t = t + 3
    b = b + 3

    first_core = mp == 0
    owned, others = [], []
    for n in (0, 4):
        owned.append(jnp.sum(qkv[n].astype(jnp.float32), axis=0, keepdims=True))
        others.append(jnp.sum(qkv[n + 1].astype(jnp.float32), axis=0, keepdims=True))
    for row in (bias_o, gain_one, shift_one, sums_b[0:1, :], sums_b[1:2, :], sums_b[2:3, :]):
        owned.append(jnp.where(first_core, row[:, :half], row[:, half:]))
        others.append(jnp.where(first_core, row[:, half:], row[:, :half]))
    for n in range(0, tiles, 2):
        owned.append(jnp.concatenate([bias_in[n : n + 1, :part], bias_in[n + 1 : n + 2, :part]], axis=1))
        others.append(jnp.concatenate([bias_in[n : n + 1, part:], bias_in[n + 1 : n + 2, part:]], axis=1))
    fill = jnp.zeros((QUARTER - len(owned), half), jnp.float32)
    grads[last_rows : last_rows + QUARTER, :half] = jnp.concatenate(owned + [fill], axis=0).astype(jnp.bfloat16)
    send_v[...] = jnp.concatenate(others + [fill], axis=0).astype(jnp.bfloat16)
    vectors = pltpu.make_async_remote_copy(send_v, land_v, vsem, vrsem, device_id=twin, device_id_type=MESH)
    vectors.start()
    take_twin(b - 1)
    vectors.wait()
    add_into(grads.at[last_rows : last_rows + QUARTER, :half], land_v)
    to_twin(b - 2).wait_send()
    to_twin(b - 1).wait_send()
    tick(t)
    finish(third)

    def input_loop(i, carry):
        rows = pl.ds(pl.multiple_of(i * step, step), step)
        total = acc[rows, :]
        for n, ref in enumerate((buf_c, buf_d, buf_e)):
            for h in (0, 1):
                total = total + dot_nt(qkv[2 * n + h, rows, :], ref[h])
        buf_a[rows, :] = total.astype(jnp.bfloat16)
        tick(t + 1 + i)
        return carry

    lax.fori_loop(0, tokens // step, input_loop, 0)
    t = t + 1 + tokens // step
    ig_keep = pltpu.make_async_copy(buf_a.at[:, own_cols], ig_own, gsem.at[0])
    ig_send = pltpu.make_async_remote_copy(
        buf_a.at[:, other_cols], ig_recv, gsem.at[1], gsem.at[2], device_id=twin, device_id_type=MESH
    )
    ig_keep.start()
    ig_send.start()
    for gift in gifts:
        gift.wait_send()

    def end_gifts(j, carry):
        for gift in ff_gifts(j):
            gift.wait_send()
        return carry

    lax.fori_loop(0, tiles, end_gifts, 0)

    def rest(i, carry):
        tick(i)
        return carry

    lax.fori_loop(t, pairs + STAGES[-1], rest, 0)
    ig_keep.wait()
    ig_send.wait()


HBM = pl.BlockSpec(memory_space=pltpu.HBM)
VMEM = pl.BlockSpec(memory_space=pltpu.VMEM)
SMEM = pl.BlockSpec(memory_space=pltpu.SMEM)


def shape(dims, dtype=jnp.bfloat16):
    return jax.ShapeDtypeStruct(dims, dtype)


def run_layer(inputs, cotangent, w_q, w_k, w_v, w_o, w_in, w_back, vectors, lengths):
    tokens = inputs.shape[0] // 2
    half = inputs.shape[1]
    full = 2 * half
    seq = inputs.shape[0] // lengths.shape[0]
    ff_half = w_in.shape[1]
    tiles = ff_half // (BLOCK // 2)
    wide = BLOCK
    rows = (tiles + 4) * BLOCK + PAIR
    f32 = jnp.float32
    bf16 = jnp.bfloat16
    return pl.pallas_call(
        layer_kernel,
        name="layer",
        out_shape=(
            shape((rows, full)), shape((tokens, half)), shape((tokens, half)), shape((tokens, half)),
            shape((tokens, half)), shape((tiles, tokens, wide)), shape((tiles, tokens, wide)),
            shape((3, full, half)), shape((half, full)), shape((full, ff_half)), shape((ff_half, full)),
        ),
        in_specs=[HBM] * 8 + [VMEM] * 9 + [SMEM],
        out_specs=(HBM,) * 11,
        scratch_shapes=[
            pltpu.VMEM((rows, full), bf16),
            pltpu.VMEM((SLOTS, 2, 2 * QUARTER, full), bf16),
            pltpu.VMEM((SLOTS, 2, 2 * QUARTER, full), bf16),
            pltpu.VMEM((SLOTS, 2, QUARTER, full), bf16),
            pltpu.VMEM((SLOTS, 2, QUARTER, full), bf16),
            pltpu.VMEM((2, BLOCK, full), bf16),
            pltpu.VMEM((2, BLOCK, full), bf16),
            pltpu.VMEM((QUARTER, half), bf16),
            pltpu.VMEM((QUARTER, half), bf16),
            pltpu.VMEM((tokens, full), f32),
            pltpu.VMEM((tokens, full), bf16),
            pltpu.VMEM((tokens, full), bf16),
            pltpu.VMEM((2, tokens, half), bf16),
            pltpu.VMEM((2, tokens, half), bf16),
            pltpu.VMEM((2, tokens, half), bf16),
            pltpu.VMEM((2, half, full), bf16),
            pltpu.VMEM((tokens, wide), bf16),
            pltpu.VMEM((6, tokens, half), bf16),
            pltpu.VMEM((tokens, full), bf16),
            pltpu.VMEM((2, tokens, half), bf16),
            pltpu.VMEM((2, tokens, half), bf16),
            pltpu.VMEM((tokens, full), bf16),
            pltpu.VMEM((tokens, 128), f32),
            pltpu.VMEM((QUARTER, half), f32),
            pltpu.VMEM((QUARTER, half), f32),
            pltpu.VMEM((QUARTER, full), f32),
            pltpu.VMEM((8, full), f32),
            pltpu.VMEM((tiles, wide), f32),
            pltpu.VMEM((tiles, wide), f32),
            pltpu.VMEM((8, full), f32),
            pltpu.VMEM((seq, 128), bf16),
            pltpu.SemaphoreType.DMA((7, 2, SLOTS)),
            pltpu.SemaphoreType.DMA((7, 2, SLOTS)),
            pltpu.SemaphoreType.DMA((2, SLOTS)),
            pltpu.SemaphoreType.DMA((2,)),
            pltpu.SemaphoreType.DMA((2,)),
            pltpu.SemaphoreType.DMA,
            pltpu.SemaphoreType.DMA,
            pltpu.SemaphoreType.DMA((2, 6)),
            pltpu.SemaphoreType.DMA((2, 2)),
            pltpu.SemaphoreType.DMA((18,)),
            pltpu.SemaphoreType.DMA((6,)),
            pltpu.SemaphoreType.DMA((7,)),
            pltpu.SemaphoreType.DMA((7,)),
            pltpu.SemaphoreType.DMA((tiles, 2)),
            pltpu.SemaphoreType.DMA((tiles, 2)),
        ],
        compiler_params=pltpu.CompilerParams(
            collective_id=0, has_side_effects=True, vmem_limit_bytes=62 << 20
        ),
    )(inputs, cotangent, w_q, w_k, w_v, w_o, w_in, w_back, *vectors, lengths)


def unpack_kernel(
    packed, out_mine, out_got, ig_mine, ig_got,
    output, input_grad, g_q, g_k, g_v, g_o, g_in, g_back,
    loaded, wide, passed, isem, osem, csem,
):
    mp = lax.axis_index("mp")
    tokens, half = out_mine.shape
    mine = pl.ds(pl.multiple_of(mp * tokens, tokens), tokens)
    other = pl.ds(pl.multiple_of((1 - mp) * tokens, tokens), tokens)
    pieces = ((out_mine, output.at[mine]), (out_got, output.at[other]), (ig_mine, input_grad.at[mine]), (ig_got, input_grad.at[other]))
    moves = [pltpu.make_async_copy(src, passed.at[i], csem.at[0, i]) for i, (src, _) in enumerate(pieces)]
    leaves = [pltpu.make_async_copy(passed.at[i], dst, csem.at[1, i]) for i, (_, dst) in enumerate(pieces)]
    for move in moves:
        move.start()
    part = BLOCK // 2
    full = packed.shape[1]
    tiles = g_back.shape[0] // part
    blocks = tiles + 4

    def fetch(b):
        return pltpu.make_async_copy(packed.at[b * BLOCK : (b + 1) * BLOCK], loaded.at[b % 2], isem.at[b % 2])

    def stores(b):
        ref = wide.at[b % 2]
        if b < tiles:
            pieces = [(ref.at[:part], g_back.at[(tiles - 1 - b) * part : (tiles - b) * part])]
            for c in range(0, full, part):
                pieces.append((ref.at[part:, c : c + part], g_in.at[c : c + part, (tiles - 1 - b) * part : (tiles - b) * part]))
        elif b == tiles:
            pieces = [(ref, g_o)]
        else:
            target = (g_q, g_k, g_v)[b - tiles - 1]
            pieces = [(ref.at[:, :half], target.at[:half]), (ref.at[:, half:], target.at[half:])]
        return [pltpu.make_async_copy(src, dst, osem.at[b % 2, i]) for i, (src, dst) in enumerate(pieces)]

    fetch(0).start()
    for move, leave in zip(moves, leaves):
        move.wait()
        leave.start()
    for b in range(blocks):
        if b + 1 < blocks:
            fetch(b + 1).start()
        fetch(b).wait()
        if b >= 2:
            for store in stores(b - 2):
                store.wait()
        for r in range(0, BLOCK, CHUNK):
            wide[b % 2, r : r + CHUNK, :] = loaded[b % 2, r : r + CHUNK, :].astype(jnp.float32)
        for store in stores(b):
            store.start()
    for b in (blocks - 2, blocks - 1):
        for store in stores(b):
            store.wait()
    for leave in leaves:
        leave.wait()


def run_unpack(packed, out_mine, out_got, ig_mine, ig_got, tiles):
    tokens, half = out_mine.shape
    full = 2 * half
    ff_half = tiles * (BLOCK // 2)
    f32 = jnp.float32
    return pl.pallas_call(
        unpack_kernel,
        name="unpack",
        out_shape=(
            shape((2 * tokens, half)), shape((2 * tokens, half)),
            shape((full, half), f32), shape((full, half), f32), shape((full, half), f32), shape((half, full), f32),
            shape((full, ff_half), f32), shape((ff_half, full), f32),
        ),
        in_specs=[HBM] * 5,
        out_specs=(HBM,) * 8,
        scratch_shapes=[
            pltpu.VMEM((2, BLOCK, full), jnp.bfloat16),
            pltpu.VMEM((2, BLOCK, full), f32),
            pltpu.VMEM((4, tokens, half), jnp.bfloat16),
            pltpu.SemaphoreType.DMA((2,)),
            pltpu.SemaphoreType.DMA((2, 5)),
            pltpu.SemaphoreType.DMA((2, 4)),
        ],
        compiler_params=pltpu.CompilerParams(vmem_limit_bytes=60 << 20),
        cost_estimate=pl.CostEstimate(flops=0, bytes_accessed=60 << 20, transcendentals=0),
    )(packed, out_mine, out_got, ig_mine, ig_got)


def on_core(
    inputs, lengths, w_query, b_query, w_key, w_value, b_value, w_out, b_out, gain_one, shift_one, w_in, b_in, w_back,
    b_back, gain_two, shift_two, cotangent,
):
    half = inputs.shape[1]
    tiles = w_in.shape[1] // (BLOCK // 2)
    vectors = (b_query, b_value, b_in, b_out, gain_one, shift_one, b_back, gain_two, shift_two)
    packed, out_mine, out_got, ig_mine, ig_got, *_ = run_layer(
        inputs, cotangent, w_query, w_key, w_value, w_out, w_in, w_back, vectors, lengths
    )
    output, input_grad, g_q, g_k, g_v, g_o, g_in, g_back = run_unpack(packed, out_mine, out_got, ig_mine, ig_got, tiles)
    at = (tiles + 4) * BLOCK
    v = packed[at : at + 12, :half].astype(jnp.float32)
    return (
        output, input_grad, g_q, v[0], g_k, g_v, v[1], g_o, v[2], v[3], v[4], g_in, v[8:12].reshape(-1), g_back, v[5],
        v[6], v[7],
    )


def gelu_exact(ffn_inner):
    return jax.nn.gelu(ffn_inner, approximate=False)


def normalize_rows(summed, gain_vec, shift_vec):
    average = jnp.mean(summed, axis=-1, keepdims=True)
    centred = summed - average
    inv_std = lax.rsqrt(jnp.mean(centred * centred, axis=-1, keepdims=True) + eps)
    normed = centred * inv_std
    return (normed * gain_vec + shift_vec, normed, inv_std)


def normalize_back(grad_out, normed, inv_std, gain_vec):
    scaled = grad_out * gain_vec
    centred = scaled - jnp.mean(scaled, axis=-1, keepdims=True)
    return inv_std * (centred - normed * jnp.mean(scaled * normed, axis=-1, keepdims=True))


def on_device(
    inputs,
    lengths,
    w_query,
    b_query,
    w_key,
    w_value,
    b_value,
    w_out,
    b_out,
    gain_one,
    shift_one,
    w_in,
    b_in,
    w_back,
    b_back,
    gain_two,
    shift_two,
    cotangent,
):
    token_count, part_cols = inputs.shape
    page_count = lengths.shape[0]
    seq_len = token_count // page_count
    head_size = HDIM
    local_heads = w_query.shape[1] // head_size
    score_scale = head_size ** (-0.5)
    offset = lax.axis_index("mp") * part_cols

    def own_cols(full_array):
        return lax.dynamic_slice_in_dim(full_array, offset, part_cols, full_array.ndim - 1)

    vectors = jnp.stack([b_out, gain_one, shift_one, b_back, gain_two, shift_two])
    token_rows, vector_rows = (
        lax.all_gather(inputs, "mp", axis=1, tiled=True),
        lax.all_gather(vectors, "mp", axis=1, tiled=True),
    )
    vector_rows = vector_rows.astype(jnp.float32)
    full_b_out, full_gain_one, full_shift_one = (vector_rows[0], vector_rows[1], vector_rows[2])
    full_b_back, full_gain_two, full_shift_two = (vector_rows[3], vector_rows[4], vector_rows[5])
    positions = jnp.arange(seq_len, dtype=jnp.int32)
    key_valid = positions[None, :] < lengths[:, None]
    row_valid = key_valid.reshape(token_count, 1).astype(jnp.float32)
    head_shape = (page_count, seq_len, local_heads, head_size)
    queries = (
        (
            jnp.dot(token_rows, w_query, preferred_element_type=jnp.float32)
            + b_query.astype(jnp.float32)
        )
        .astype(jnp.bfloat16)
        .reshape(head_shape)
    )
    keys_all = (
        jnp.dot(token_rows, w_key, preferred_element_type=jnp.float32)
        .astype(jnp.bfloat16)
        .reshape(head_shape)
    )
    values = (
        (
            jnp.dot(token_rows, w_value, preferred_element_type=jnp.float32)
            + b_value.astype(jnp.float32)
        )
        .astype(jnp.bfloat16)
        .reshape(head_shape)
    )

    def masked_scores(page_queries, page_keys, page_valid):
        scores = (
            jnp.einsum("qhd,khd->hqk", page_queries, page_keys, preferred_element_type=jnp.float32)
            * score_scale
        )
        return jnp.where(page_valid[None, None, :], scores, -1e30)

    def attend(packed):
        page_queries, page_keys, page_values, page_valid = packed
        scores = masked_scores(page_queries, page_keys, page_valid)
        row_max = jnp.max(scores, axis=-1, keepdims=True)
        shifted = jnp.exp(scores - row_max)
        row_sum = jnp.sum(shifted, axis=-1, keepdims=True)
        weights = (shifted / row_sum).astype(jnp.bfloat16)
        context = jnp.einsum(
            "hqk,khd->qhd", weights, page_values, preferred_element_type=jnp.float32
        )
        return (context.astype(jnp.bfloat16), (row_max + jnp.log(row_sum))[..., 0])

    context, log_total = lax.map(attend, (queries, keys_all, values, key_valid))
    context = context.reshape(token_count, local_heads * head_size)
    attn_part = jnp.dot(context, w_out, preferred_element_type=jnp.float32)
    attended = token_rows.astype(jnp.float32) + lax.psum(attn_part, "mp") + full_b_out
    hidden_one, normed_one, inv_std_one = normalize_rows(attended, full_gain_one, full_shift_one)
    hidden_low = hidden_one.astype(jnp.bfloat16)
    ffn_inner = jnp.dot(hidden_low, w_in, preferred_element_type=jnp.float32) + b_in.astype(
        jnp.float32
    )
    gelu_value, gelu_pull = jax.vjp(gelu_exact, ffn_inner)
    activated = gelu_value.astype(jnp.bfloat16)
    ffn_part = jnp.dot(activated, w_back, preferred_element_type=jnp.float32)
    summed = hidden_one + lax.psum(ffn_part, "mp") + full_b_back
    out_full, normed_two, inv_std_two = normalize_rows(summed, full_gain_two, full_shift_two)
    output = own_cols(out_full).astype(jnp.bfloat16)
    grad_out = lax.all_gather(cotangent, "mp", axis=1, tiled=True).astype(jnp.float32) * row_valid
    grad_summed = normalize_back(grad_out, normed_two, inv_std_two, full_gain_two)
    grad_gain_two = own_cols(jnp.sum(grad_out * normed_two, axis=0))
    grad_shift_two = own_cols(jnp.sum(grad_out, axis=0))
    grad_b_back = own_cols(jnp.sum(grad_summed, axis=0))
    round_summed = grad_summed.astype(jnp.bfloat16)
    grad_act = jnp.einsum("rd,fd->rf", round_summed, w_back, preferred_element_type=jnp.float32)
    grad_inner = gelu_pull(grad_act)[0].astype(jnp.bfloat16)
    grad_w_back = jnp.einsum(
        "rf,rd->fd", activated, round_summed, preferred_element_type=jnp.float32
    )
    grad_w_in = jnp.einsum("rd,rf->df", hidden_low, grad_inner, preferred_element_type=jnp.float32)
    grad_b_in = jnp.sum(grad_inner.astype(jnp.float32), axis=0)
    ffn_grads = (grad_w_in, grad_b_in, grad_w_back, grad_b_back, grad_gain_two, grad_shift_two)
    back_part = jnp.einsum("rf,df->rd", grad_inner, w_in, preferred_element_type=jnp.float32)
    grad_hidden = lax.psum(back_part, "mp") + grad_summed
    grad_gain_one = own_cols(jnp.sum(grad_hidden * normed_one, axis=0))
    grad_shift_one = own_cols(jnp.sum(grad_hidden, axis=0))
    grad_attended = normalize_back(grad_hidden, normed_one, inv_std_one, full_gain_one)
    grad_b_out = own_cols(jnp.sum(grad_attended, axis=0))
    own_attended = own_cols(grad_attended)
    round_attended = grad_attended.astype(jnp.bfloat16)
    grad_w_out = jnp.einsum(
        "rc,rd->cd", context, round_attended, preferred_element_type=jnp.float32
    )
    grad_context = (
        jnp.einsum("rd,cd->rc", round_attended, w_out, preferred_element_type=jnp.float32)
        .astype(jnp.bfloat16)
        .reshape(head_shape)
    )

    def attend_back(packed):
        page_queries, page_keys, page_values, page_valid, page_total, page_grad = packed
        scores = masked_scores(page_queries, page_keys, page_valid)
        probabilities = jnp.exp(scores - page_total[..., None])
        weights = probabilities.astype(jnp.bfloat16)
        grad_values = jnp.einsum(
            "hqk,qhd->khd", weights, page_grad, preferred_element_type=jnp.float32
        )
        grad_weights = jnp.einsum(
            "qhd,khd->hqk", page_grad, page_values, preferred_element_type=jnp.float32
        )
        grad_scores = (
            probabilities
            * (grad_weights - jnp.sum(probabilities * grad_weights, axis=-1, keepdims=True))
        ).astype(jnp.bfloat16)
        grad_queries = (
            jnp.einsum("hqk,khd->qhd", grad_scores, page_keys, preferred_element_type=jnp.float32)
            * score_scale
        )
        grad_keys = (
            jnp.einsum(
                "hqk,qhd->khd", grad_scores, page_queries, preferred_element_type=jnp.float32
            )
            * score_scale
        )
        return (
            grad_queries.astype(jnp.bfloat16),
            grad_keys.astype(jnp.bfloat16),
            grad_values.astype(jnp.bfloat16),
        )

    grad_queries, grad_keys, grad_values = lax.map(
        attend_back, (queries, keys_all, values, key_valid, log_total, grad_context)
    )
    grad_queries = grad_queries.reshape(token_count, local_heads * head_size)
    grad_keys = grad_keys.reshape(token_count, local_heads * head_size)
    grad_values = grad_values.reshape(token_count, local_heads * head_size)
    grad_w_query = jnp.einsum(
        "rd,rc->dc", token_rows, grad_queries, preferred_element_type=jnp.float32
    )
    grad_w_key = jnp.einsum("rd,rc->dc", token_rows, grad_keys, preferred_element_type=jnp.float32)
    grad_w_value = jnp.einsum(
        "rd,rc->dc", token_rows, grad_values, preferred_element_type=jnp.float32
    )
    grad_b_query = jnp.sum(grad_queries.astype(jnp.float32), axis=0)
    grad_b_value = jnp.sum(grad_values.astype(jnp.float32), axis=0)
    input_part = (
        jnp.einsum("rc,dc->rd", grad_queries, w_query, preferred_element_type=jnp.float32)
        + jnp.einsum("rc,dc->rd", grad_keys, w_key, preferred_element_type=jnp.float32)
        + jnp.einsum("rc,dc->rd", grad_values, w_value, preferred_element_type=jnp.float32)
    )
    input_grad = (
        lax.psum_scatter(
            input_part.astype(jnp.bfloat16), "mp", scatter_dimension=1, tiled=True
        ).astype(jnp.float32)
        + own_attended
    ).astype(jnp.bfloat16)
    all_grads = (
        lax.psum(grad_w_query.astype(jnp.bfloat16), "dp").astype(jnp.float32),
        lax.psum(grad_b_query.astype(jnp.bfloat16), "dp").astype(jnp.float32),
        lax.psum(grad_w_key.astype(jnp.bfloat16), "dp").astype(jnp.float32),
        lax.psum(grad_w_value.astype(jnp.bfloat16), "dp").astype(jnp.float32),
        lax.psum(grad_b_value.astype(jnp.bfloat16), "dp").astype(jnp.float32),
        lax.psum(grad_w_out.astype(jnp.bfloat16), "dp").astype(jnp.float32),
        lax.psum(grad_b_out.astype(jnp.bfloat16), "dp").astype(jnp.float32),
        lax.psum(grad_gain_one.astype(jnp.bfloat16), "dp").astype(jnp.float32),
        lax.psum(grad_shift_one.astype(jnp.bfloat16), "dp").astype(jnp.float32),
        lax.psum(grad_w_in.astype(jnp.bfloat16), "dp").astype(jnp.float32),
        lax.psum(grad_b_in.astype(jnp.bfloat16), "dp").astype(jnp.float32),
        lax.psum(grad_w_back.astype(jnp.bfloat16), "dp").astype(jnp.float32),
        lax.psum(grad_b_back.astype(jnp.bfloat16), "dp").astype(jnp.float32),
        lax.psum(grad_gain_two.astype(jnp.bfloat16), "dp").astype(jnp.float32),
        lax.psum(grad_shift_two.astype(jnp.bfloat16), "dp").astype(jnp.float32),
    )
    attn_grads = all_grads[:9]
    ffn_grads = all_grads[9:]
    return (
        output,
        input_grad,
        attn_grads[0],
        attn_grads[1],
        attn_grads[2],
        attn_grads[3],
        attn_grads[4],
        attn_grads[5],
        attn_grads[6],
        attn_grads[7],
        attn_grads[8],
        ffn_grads[0],
        ffn_grads[1],
        ffn_grads[2],
        ffn_grads[3],
        ffn_grads[4],
        ffn_grads[5],
    )


def solution(mesh):
    placed = (
        P("dp", "mp"),
        P("dp"),
        P(None, "mp"),
        P("mp"),
        P(None, "mp"),
        P(None, "mp"),
        P("mp"),
        P("mp", None),
        P("mp"),
        P("mp"),
        P("mp"),
        P(None, "mp"),
        P("mp"),
        P("mp", None),
        P("mp"),
        P("mp"),
        P("mp"),
        P("dp", "mp"),
    )
    return jax.shard_map(
        on_core if dict(mesh.shape) == {"dp": 16, "mp": 2} else on_device,
        mesh=mesh,
        in_specs=placed,
        out_specs=(
            P("dp", "mp"),
            P("dp", "mp"),
            P(None, "mp"),
            P("mp"),
            P(None, "mp"),
            P(None, "mp"),
            P("mp"),
            P("mp", None),
            P("mp"),
            P("mp"),
            P("mp"),
            P(None, "mp"),
            P("mp"),
            P("mp", None),
            P("mp"),
            P("mp"),
            P("mp"),
        ),
        check_vma=False,
    )
```

profile of v0, /device:TPU:0, one launch (start us, length us, event | category | flops | bytes accessed | tf_op | source)
XLA Modules:
  0.0 305.9 jit_solution(7049393597144804029)
XLA Ops:
  0.7 287.0 %layer.1 = (bf16[6272,1024]{1,0:T(8,128)(2,1)}, bf16[1024,512]{1,0:T(8,128)(2,1)}, bf16[1024,512]{1,0:T(8,128)(2,1)}, bf16[1024,512]{1,0:T(8,128)(2,1)}, bf16[10...) custom-call(bf16[2048,512]{1,0:T(8,128)(2,1)} %inputs.1, ...), custom_call_target="tpu_custom_call" | custom-call | tf_op jit(solution)/shard_map/layer/pallas_call | solution.py:781
  287.6 16.3 %unpack.1 = (bf16[2048,512]{1,0:T(8,128)(2,1)}, bf16[2048,512]{1,0:T(8,128)(2,1)}, f32[1024,512]{1,0:T(8,128)}, f32[1024,512]{1,0:T(8,128)}, f32[1024,512]{1,0:T...) custom-call(bf16[6272,1024]{1,0:T(8,128)(2,1)} %get-tuple-element.30.packed, ...), custom_call_target="tpu_custom_call" | custom-call | bytes 62914560 | tf_op jit(solution)/shard_map/unpack/pallas_call | solution.py:907
  303.9 0.7 slice_convert_fusion
  304.7 0.6 fusion
  305.3 0.6 copy.35
  (1 shorter events, 0.0 us)
where the time goes:
time: 306 us
  Pallas kernels  303 us (99%)
    pallas_call x1, Pallas kernels, run_layer(): pl.pallas_call(layer_kernel, name='layer', out_shape=(shape((rows, full))...  287 us
    pallas_call x1, Pallas kernels, run_unpack(): pl.pallas_call(unpack_kernel, name='unpack', out_shape=(shape((2 * tokens...  16.3 us

commit v1 on v0

--- a/solution.py
+++ b/solution.py
@@ -20,21 +20,23 @@
 CHUNK = 4 * QUARTER
 PAIR = 2 * CHUNK
 BLOCK = 4 * PAIR
-SLOTS = 16
-STAGES = (0, 2, 4, 6, 8, 10, 12, 14)
+SLOTS = (6, 6, 4, 6, 8, 6, 4, 6, 10)
+KEEP_SLOTS = 4
+HOPS = (3, 2, 2, 2, 2, 2, 2, 2, 3)
 
 
 def rows_at(start, size):
     return pl.ds(pl.multiple_of(start, QUARTER), size)
 
 
-def chip_sum(pairs, grads, out, land_a, land_z, land_m, land_b, ssem, rsem, osem):
+def chip_sum(pairs, grads, out, lands, ssem, rsem, osem):
     dp = lax.axis_index("dp")
     mp = lax.axis_index("mp")
     z, y, x = dp // 4, (dp // 2) % 2, dp % 2
     inner = (z == 1) | (z == 2)
     outer = jnp.logical_not(inner)
-    quarter = jnp.where(z == 1, 0, 1)
+    upper = z >= 2
+    cols = grads.shape[1] // 4
 
     def chip(cz, cy, cx):
         return (cz * 4 + cy * 2 + cx, mp)
@@ -47,21 +49,22 @@
     across = chip(3 - z, y, x)
     twin = (dp, 1 - mp)
 
+    line_peer = chip(z + 1 - 2 * lax.rem(z, 2), y, x)
+
     def meet():
         barrier = pltpu.get_barrier_semaphore()
-        for peer in first_peer + (twin,):
+        for peer in first_peer + (twin, line_peer, across):
             pl.semaphore_signal(barrier, 1, device_id=peer, device_id_type=MESH)
-
-        @pl.when(inner)
-        def _():
-            for peer in (outward, across):
-                pl.semaphore_signal(barrier, 1, device_id=peer, device_id_type=MESH)
-            pl.semaphore_wait(barrier, 5)
-
-        @pl.when(outer)
-        def _():
-            pl.semaphore_signal(barrier, 1, device_id=inward, device_id_type=MESH)
-            pl.semaphore_wait(barrier, 4)
+        pl.semaphore_wait(barrier, 5)
+
+    def at_cols(start, count):
+        return pl.ds(pl.multiple_of(start * cols, cols), count * cols)
+
+    mine = at_cols(z, 1)
+    three = at_cols(jnp.where(upper, 0, 1), 3)
+    near_two = at_cols(jnp.where(upper, 2, 0), 2)
+    far_two = at_cols(jnp.where(upper, 0, 2), 2)
+    end_one = at_cols(jnp.where(upper, 3, 0), 1)
 
     def half(ref, kind, k, which):
         return ref.at[rows_at(k * PAIR + kind * CHUNK + which * 2 * QUARTER, 2 * QUARTER)]
@@ -72,128 +75,171 @@
     def own_out(kind, k):
         return half(out, kind, k, side[kind])
 
-    def part_of(ref, kind, k, which):
-        return ref.at[rows_at(k * PAIR + kind * CHUNK + (side[kind] * 2 + which) * QUARTER, QUARTER)]
-
-    def part(kind, k, which):
-        return part_of(grads, kind, k, which)
-
     def keep(kind, k):
         return pltpu.make_async_copy(
-            part(kind, k, quarter), part_of(out, kind, k, quarter), osem.at[kind, lax.rem(k, SLOTS)]
-        )
+            own(kind, k).at[:, mine], own_out(kind, k).at[:, mine], osem.at[kind, lax.rem(k, KEEP_SLOTS)]
+        )
+
+    def land(stage, kind, k):
+        return lands[stage].at[lax.rem(k, SLOTS[stage]), kind]
 
     def send(stage, kind, k, source, target, peer):
-        slot = lax.rem(k, SLOTS)
+        slot = sum(SLOTS[:stage]) + lax.rem(k, SLOTS[stage])
         return pltpu.make_async_remote_copy(
             source,
             target,
-            ssem.at[stage, kind, slot],
-            rsem.at[stage, kind, slot],
+            ssem.at[kind, slot],
+            rsem.at[kind, slot],
             device_id=peer,
             device_id_type=MESH,
         )
 
-    def landing(buffer, kind, k):
-        return buffer.at[lax.rem(k, SLOTS), kind]
-
     def scatter_first(kind, k):
-        return send(0, kind, k, half(grads, kind, k, 1 - side[kind]), landing(land_a, kind, k), first_peer[kind])
+        return send(0, kind, k, half(grads, kind, k, 1 - side[kind]), land(0, kind, k), first_peer[kind])
 
     def go_in(kind, k):
-        return send(1, kind, k, own(kind, k), landing(land_z, kind, k), inward)
-
-    def scatter_across(kind, k):
-        return send(2, kind, k, part(kind, k, 1 - quarter), landing(land_m, kind, k), across)
+        return send(1, kind, k, own(kind, k).at[:, three], land(1, kind, k).at[:, three], inward)
+
+    def go_across(kind, k):
+        return send(2, kind, k, own(kind, k).at[:, far_two], land(2, kind, k), across)
+
+    def go_out(kind, k):
+        return send(3, kind, k, own(kind, k).at[:, end_one], land(3, kind, k), outward)
 
     def swap_second(kind, k):
-        return send(3, kind, k, part(kind, k, quarter), landing(land_b, kind, k), second_peer[kind])
-
-    def gather_across(kind, k):
-        return send(4, kind, k, part(kind, k, quarter), part_of(out, kind, k, quarter), across)
-
-    def go_out(kind, k):
-        return send(5, kind, k, own_out(kind, k), own_out(kind, k), outward)
+        return send(4, kind, k, own(kind, k).at[:, mine], land(4, kind, k), second_peer[kind])
+
+    def back_in(kind, k):
+        return send(5, kind, k, own_out(kind, k).at[:, mine], own_out(kind, k).at[:, mine], inward)
+
+    def back_across(kind, k):
+        return send(6, kind, k, own_out(kind, k).at[:, near_two], own_out(kind, k).at[:, near_two], across)
+
+    def back_out(kind, k):
+        return send(7, kind, k, own_out(kind, k).at[:, three], own_out(kind, k).at[:, three], outward)
 
     def gather_first(kind, k):
-        return send(6, kind, k, own_out(kind, k), own_out(kind, k), first_peer[kind])
+        return send(8, kind, k, own_out(kind, k), own_out(kind, k), first_peer[kind])
+
+    offsets = [0]
+    for hop in HOPS:
+        offsets.append(offsets[-1] + hop)
 
     def step(t):
-        ks = [t - offset for offset in STAGES]
+        ks = [t - offset for offset in offsets]
         live = [(k >= 0) & (k < pairs) for k in ks]
 
-        @pl.when(live[7])
-        def _():
-            for kind in (0, 1):
-                gather_first(kind, ks[7]).wait()
-
-        @pl.when(live[6] & inner)
-        def _():
-            for kind in (0, 1):
-                go_out(kind, ks[6]).wait_send()
-
-        @pl.when(live[6] & outer)
-        def _():
-            for kind in (0, 1):
-                go_out(kind, ks[6]).wait_recv()
-                gather_first(kind, ks[6]).start()
-
-        @pl.when(live[5] & inner)
-        def _():
-            for kind in (0, 1):
-                gather_across(kind, ks[5]).wait()
+        def when(n, who=None):
+            return pl.when(live[n] if who is None else live[n] & who)
+
+        @when(9)
+        def _():
+            for kind in (0, 1):
+                gather_first(kind, ks[9]).wait()
+
+        @when(8, inner)
+        def _():
+            for kind in (0, 1):
+                back_out(kind, ks[8]).wait_send()
+
+        @when(8, outer)
+        def _():
+            for kind in (0, 1):
+                back_out(kind, ks[8]).wait_recv()
+                gather_first(kind, ks[8]).start()
+
+        @when(7, inner)
+        def _():
+            for kind in (0, 1):
+                back_across(kind, ks[7]).wait()
+                back_out(kind, ks[7]).start()
+                gather_first(kind, ks[7]).start()
+
+        @when(6, inner)
+        def _():
+            for kind in (0, 1):
+                back_in(kind, ks[6]).wait_recv()
+                keep(kind, ks[6]).wait()
+                back_across(kind, ks[6]).start()
+
+        @when(6, outer)
+        def _():
+            for kind in (0, 1):
+                back_in(kind, ks[6]).wait_send()
+
+        @when(5)
+        def _():
+            for kind in (0, 1):
+                swap_second(kind, ks[5]).wait()
+                add_into(own(kind, ks[5]).at[:, mine], land(4, kind, ks[5]))
+                keep(kind, ks[5]).start()
+
+        @when(5, outer)
+        def _():
+            for kind in (0, 1):
                 keep(kind, ks[5]).wait()
-                go_out(kind, ks[5]).start()
-                gather_first(kind, ks[5]).start()
-
-        @pl.when(live[4] & inner)
-        def _():
-            for kind in (0, 1):
-                swap_second(kind, ks[4]).wait()
-                add_into(part(kind, ks[4], quarter), landing(land_b, kind, ks[4]))
-                gather_across(kind, ks[4]).start()
-                keep(kind, ks[4]).start()
-
-        @pl.when(live[3] & inner)
-        def _():
-            for kind in (0, 1):
-                scatter_across(kind, ks[3]).wait()
-                add_into(part(kind, ks[3], quarter), landing(land_m, kind, ks[3]))
+                back_in(kind, ks[5]).start()
+
+        @when(4, outer)
+        def _():
+            for kind in (0, 1):
+                go_out(kind, ks[4]).wait_recv()
+                add_into(own(kind, ks[4]).at[:, mine], land(3, kind, ks[4]))
+                swap_second(kind, ks[4]).start()
+
+        @when(4, inner)
+        def _():
+            for kind in (0, 1):
+                go_out(kind, ks[4]).wait_send()
+
+        @when(3, inner)
+        def _():
+            for kind in (0, 1):
+                go_across(kind, ks[3]).wait()
+                add_into(own(kind, ks[3]).at[:, near_two], land(2, kind, ks[3]))
+                go_out(kind, ks[3]).start()
                 swap_second(kind, ks[3]).start()
 
-        @pl.when(live[2] & inner)
+        @when(2, inner)
         def _():
             for kind in (0, 1):
                 go_in(kind, ks[2]).wait_recv()
-                add_into(own(kind, ks[2]), landing(land_z, kind, ks[2]))
-                scatter_across(kind, ks[2]).start()
-
-        @pl.when(live[2] & outer)
+                add_into(own(kind, ks[2]).at[:, three], land(1, kind, ks[2]).at[:, three])
+                go_across(kind, ks[2]).start()
+
+        @when(2, outer)
         def _():
             for kind in (0, 1):
                 go_in(kind, ks[2]).wait_send()
 
-        @pl.when(live[1])
+        @when(1)
         def _():
             for kind in (0, 1):
                 scatter_first(kind, ks[1]).wait()
-                add_into(own(kind, ks[1]), landing(land_a, kind, ks[1]))
-
-                @pl.when(outer)
-                def _():
-                    go_in(kind, ks[1]).start()
-
-        @pl.when(live[0])
+                add_into(own(kind, ks[1]), land(0, kind, ks[1]))
+
+        @when(1, outer)
+        def _():
+            for kind in (0, 1):
+                go_in(kind, ks[1]).start()
+
+        @when(0)
         def _():
             for kind in (0, 1):
                 scatter_first(kind, ks[0]).start()
 
-    return meet, step
+    return meet, step, pairs + offsets[-1], (twin,) + first_peer + (line_peer, across)
 
 
 def add_into(target, arrived):
     total = target[...].astype(jnp.float32) + arrived[...].astype(jnp.float32)
     target[...] = total.astype(jnp.bfloat16)
+
+
+def land_shapes(full):
+    two = 2 * QUARTER
+    wide = (full, full, full // 2, full // 4, full // 4)
+    return [pltpu.VMEM((slots, 2, two, n), jnp.bfloat16) for slots, n in zip(SLOTS, wide)]
 
 
 def dot_tn(left, right):
@@ -218,6 +264,15 @@
     return lax.broadcasted_iota(jnp.int32, (rows, 128), 1)
 
 
+def spread_lanes(value, lane, other):
+    first = value.astype(jnp.bfloat16)
+    rest = value - first.astype(jnp.float32)
+    second = rest.astype(jnp.bfloat16)
+    third = (rest - second.astype(jnp.float32)).astype(jnp.bfloat16)
+    at = lane % 64
+    return jnp.where(at == 0, first, jnp.where(at == 1, second, jnp.where(at == 2, third, other)))
+
+
 def key_lanes(length, rows):
     lane = lane_of(rows) % 64
     slot = lax.broadcasted_iota(jnp.int32, (rows, 128), 0)
@@ -228,13 +283,14 @@
 def layer_kernel(
     inputs, cotangent, w_q, w_k, w_v, w_o, w_in, w_back,
     b_q, b_v, b_in, b_o, g_one, s_one, b_back, g_two, s_two, lens,
-    out, out_own, out_recv, ig_own, ig_recv, act_hbm, slope_hbm, w_other, w_oo, w_ino, w_backo,
-    grads, land_a, land_z, land_m, land_b, send_t, land_t, send_v, land_v, acc, buf_a, low, buf_c, buf_d, buf_e,
+    out, vec_out, out_own, out_recv, ig_own, ig_recv, act_hbm, slope_hbm, w_other, w_oo, w_ino, w_backo,
+    grads, land_0, land_1, land_2, land_3, land_4, send_t, land_t, vec_sum, vec_land, acc, buf_a, low, buf_c, buf_d, buf_e,
     buf_f, inner_g, qkv, xb, ctx, aux, normed_b, inv_b, vec_own, vec_oth, nat, bias_qkv, bias_ff, bias_in, sums_b, kl,
     ssem, rsem, osem, tsem, trsem, vsem, vrsem, isem, psem, lsem, gsem, xsem, xrsem, fsem, frsem,
 ):
     dp = lax.axis_index("dp")
     mp = lax.axis_index("mp")
+    lands = (land_0, land_1, land_2, land_3, land_4)
     tokens, full = buf_a.shape
     half = full // 2
     tiles = act_hbm.shape[0]
@@ -243,8 +299,7 @@
     seq = kl.shape[0]
     pages = tokens // seq
     pairs = grads.shape[0] // PAIR
-    last_rows = (pairs - 1) * PAIR
-    meet, tick = chip_sum(pairs, grads, out, land_a, land_z, land_m, land_b, ssem, rsem, osem)
+    meet, tick, last_tick, swap_peers = chip_sum(pairs, grads, out, lands, ssem, rsem, osem)
     own_cols = pl.ds(pl.multiple_of(mp * half, half), half)
     other_cols = pl.ds(pl.multiple_of((1 - mp) * half, half), half)
     own_tokens = pl.ds(pl.multiple_of(mp * tokens, tokens), tokens)
@@ -318,21 +373,24 @@
     loads[0].wait()
     gifts[0].wait_recv()
 
+    def project(n, h):
+        at = slice(h * half, (h + 1) * half)
+        made = jnp.dot(xb[...], grads[n * full : (n + 1) * full, at], preferred_element_type=jnp.float32)
+        qkv[2 * n + h] = (made + bias_qkv[n : n + 1, at]).astype(jnp.bfloat16)
+
     for n in range(3):
         loads[1 + n].wait()
+        project(n, 0)
+    for n in range(3):
         gifts[2 + n].wait_recv()
-        if n == 2:
-            def start_gifts(j, carry):
-                for gift in ff_gifts(j):
-                    gift.start()
-                return carry
-
-            lax.fori_loop(0, tiles, start_gifts, 0)
-
-        for h in (0, 1):
-            at = slice(h * half, (h + 1) * half)
-            made = jnp.dot(xb[...], grads[n * full : (n + 1) * full, at], preferred_element_type=jnp.float32)
-            qkv[2 * n + h] = (made + bias_qkv[n : n + 1, at]).astype(jnp.bfloat16)
+        project(n, 1)
+
+    def start_gifts(j, carry):
+        for gift in ff_gifts(j):
+            gift.start()
+        return carry
+
+    lax.fori_loop(0, tiles, start_gifts, 0)
 
     keeps = [load(6 + n, grads.at[weight_rows(n), pl.ds(half, half)], w_other.at[n]) for n in range(3)]
     for copy in keeps:
@@ -344,6 +402,7 @@
 
     lane = lane_of(seq)
     low_lanes = lane < 64
+    high_lanes = lane >= 64
     q_one = jnp.where(lane % 64 == 3, 1.0, 0.0).astype(jnp.bfloat16)
 
     def pair_forward(i, carry):
@@ -371,12 +430,7 @@
         total = jnp.where(low_lanes, out1, out0)
         value = jnp.where(low_lanes, out0, out1) / pltpu.roll(total, 64, 1)
         neg = -(jnp.where(low_lanes, top1, top0) + jnp.log(total))
-        first = neg.astype(jnp.bfloat16)
-        rest = neg - first.astype(jnp.float32)
-        second = rest.astype(jnp.bfloat16)
-        third = (rest - second.astype(jnp.float32)).astype(jnp.bfloat16)
-        at = lane % 64
-        mixed = jnp.where(at == 0, first, jnp.where(at == 1, second, jnp.where(at == 2, third, q_one)))
+        mixed = spread_lanes(neg, lane, q_one)
         ctx[side, rows, cols] = value.astype(jnp.bfloat16)
         aux[side, rows, cols] = mixed
         return carry
@@ -462,14 +516,12 @@
         def _():
             finish(saves(j - 2, slot))
 
-        for r in range(0, tokens, half):
-            rows = pl.ds(r, half)
-            inner = jnp.dot(low[rows, :], buf_e[slot], preferred_element_type=jnp.float32) + bias_ff[pl.ds(j, 1), :]
-            value, grad = gelu_and_slope(inner)
-            value = value.astype(jnp.bfloat16)
-            buf_c[slot, rows, :] = value
-            buf_d[slot, rows, :] = grad.astype(jnp.bfloat16)
-            acc[rows, :] += jnp.dot(value, buf_f[slot], preferred_element_type=jnp.float32)
+        inner = jnp.dot(low[...], buf_e[slot], preferred_element_type=jnp.float32) + bias_ff[pl.ds(j, 1), :]
+        value, grad = gelu_and_slope(inner)
+        value = value.astype(jnp.bfloat16)
+        buf_c[slot] = value
+        buf_d[slot] = grad.astype(jnp.bfloat16)
+        acc[...] += jnp.dot(value, buf_f[slot], preferred_element_type=jnp.float32)
         start(saves(j, slot))
         return carry
 
@@ -516,23 +568,41 @@
     )
     out_keep.start()
     out_send.start()
-    grads[last_rows : last_rows + PAIR, :] = jnp.zeros((PAIR, full), jnp.bfloat16)
-
-    def to_twin(b):
+
+    def to_twin(b, which):
         slot = lax.rem(b, 2)
+        at = pl.ds(which * part, part)
         return pltpu.make_async_remote_copy(
-            send_t.at[slot], land_t.at[slot], tsem.at[slot], trsem.at[slot], device_id=twin, device_id_type=MESH
-        )
+            send_t.at[slot, at],
+            land_t.at[slot, at],
+            tsem.at[slot, which],
+            trsem.at[slot, which],
+            device_id=twin,
+            device_id_type=MESH,
+        )
+
+    def give_twin(b):
+        for which in (0, 1):
+            to_twin(b, which).start()
+
+    def gave_twin(b):
+        for which in (0, 1):
+            to_twin(b, which).wait_send()
+
+    def take_half(b, which):
+        to_twin(b, which).wait_recv()
+        slot = lax.rem(b, 2)
+
+        def piece(i, carry):
+            at = which * part + i * CHUNK
+            add_into(grads.at[rows_at(b * BLOCK + at, CHUNK)], land_t.at[slot, rows_at(at, CHUNK)])
+            return carry
+
+        lax.fori_loop(0, part // CHUNK, piece, 0)
 
     def take_twin(b):
-        to_twin(b).wait_recv()
-        slot = lax.rem(b, 2)
-
-        def piece(i, carry):
-            add_into(grads.at[rows_at(b * BLOCK + i * CHUNK, CHUNK)], land_t.at[slot, rows_at(i * CHUNK, CHUNK)])
-            return carry
-
-        lax.fori_loop(0, BLOCK // CHUNK, piece, 0)
+        for which in (0, 1):
+            take_half(b, which)
 
     def backward_tile(b, carry):
         j = tiles - 1 - b
@@ -542,7 +612,7 @@
         @pl.when(b >= 2)
         def _():
             finish(fetch_made(j, slot) + fetch_in(j, slot) + fetch_back(j, slot))
-            to_twin(b - 2).wait_send()
+            gave_twin(b - 2)
 
         base = b * BLOCK
         for c in range(0, full, half):
@@ -550,26 +620,30 @@
             grads[rows_at(base, part), c : c + half] = made[:part]
             send_t[mate, :part, c : c + half] = made[part:]
 
+        to_twin(b, 0).start()
+        made = dot_nt(buf_a[...], buf_f[slot]) * buf_d[slot].astype(jnp.float32)
+        made = made.astype(jnp.bfloat16)
+        inner_g[...] = made
+        bias_in[pl.ds(j, 1), :] = jnp.sum(made.astype(jnp.float32), axis=0, keepdims=True)
+
         @pl.when(b >= 1)
         def _():
-            take_twin(b - 1)
-            tick(2 * b - 2)
-
-        total = jnp.zeros((1, wide), jnp.float32)
-        for r in range(0, tokens, half):
-            rows = pl.ds(r, half)
-            made = dot_nt(buf_a[rows, :], buf_f[slot]) * buf_d[slot, rows, :].astype(jnp.float32)
-            made = made.astype(jnp.bfloat16)
-            inner_g[rows, :] = made
-            total = total + jnp.sum(made.astype(jnp.float32), axis=0, keepdims=True)
-            acc[rows, :] += dot_nt(made, buf_e[slot])
-        bias_in[pl.ds(j, 1), :] = total
+            take_half(b - 1, 1)
+            tick(3 * b - 2)
+
+        acc[...] += dot_nt(inner_g[...], buf_e[slot])
+        take_half(b, 0)
+
+        @pl.when(b >= 1)
+        def _():
+            tick(3 * b - 1)
+
         for c in range(0, full, part):
             made = dot_tn(low[:, c : c + part], inner_g[...]).astype(jnp.bfloat16)
             grads[rows_at(base + part, part), c : c + part] = made[:, :part]
             send_t[mate, part:, c : c + part] = made[:, part:]
 
-        to_twin(b).start()
+        to_twin(b, 1).start()
 
         @pl.when(b < 2)
         def _():
@@ -579,14 +653,11 @@
         def _():
             start(fetch_made(j - 2, slot) + fetch_in(j - 2, slot) + fetch_back(j - 2, slot))
 
-        @pl.when(b >= 1)
-        def _():
-            tick(2 * b - 1)
-
+        tick(3 * b)
         return carry
 
     lax.fori_loop(0, tiles, backward_tile, 0)
-    t = 2 * tiles - 2
+    t = 3 * tiles - 2
 
     second = [load(10, w_o, buf_f.at[0]), load(11, w_oo, buf_f.at[1])]
     start(second)
@@ -611,7 +682,7 @@
     tick(t)
 
     b = tiles
-    to_twin(b - 2).wait_send()
+    gave_twin(b - 2)
     out_keep.wait()
     out_send.wait()
     finish(second)
@@ -622,8 +693,8 @@
                 grads[b * BLOCK : b * BLOCK + half, c : c + half] = made
             else:
                 send_t[b % 2, :, c : c + half] = made
-    take_twin(b - 1)
-    to_twin(b).start()
+    take_half(b - 1, 1)
+    give_twin(b)
     tick(t + 1)
     for h in (0, 1):
         for r in range(0, tokens, half):
@@ -649,26 +720,31 @@
         gp = buf_e[side, rows, cols]
         cp = ctx[side, rows, cols]
         none = jnp.zeros_like(gp)
+        product = gp.astype(jnp.float32) * cp.astype(jnp.float32)
+        sums = [jnp.sum(jnp.where(mine, product, 0.0), axis=1, keepdims=True) for mine in (low_lanes, high_lanes)]
+        shift = spread_lanes(-jnp.where(low_lanes, sums[1], sums[0]), lane, none)
         made = []
-        for h in (0, 1):
-            mine = low_lanes if h == 0 else jnp.logical_not(low_lanes)
-            scores = dot_nt(jnp.where(mine, qp, extra), jnp.where(mine, kp, kl[...]))
-            probs = jnp.exp(scores)
+        for mine in (low_lanes, high_lanes):
+            qh = jnp.where(mine, qp, none)
             gh = jnp.where(mine, gp, none)
-            grad_weights = dot_nt(gh, vp)
-            delta = jnp.sum(gh.astype(jnp.float32) * cp.astype(jnp.float32), axis=1, keepdims=True)
-            grad_scores = (probs * (grad_weights - delta)).astype(jnp.bfloat16)
-            grad_v = dot_tn(probs.astype(jnp.bfloat16), gh)
-            grad_q = jnp.dot(grad_scores, jnp.where(mine, kp, none), preferred_element_type=jnp.float32)
-            grad_k = dot_tn(grad_scores, jnp.where(mine, qp, none))
+            probs = jnp.exp(dot_nt(jnp.where(mine, kp, kl[...]), jnp.where(mine, qp, extra)))
+            grad_weights = dot_nt(jnp.where(mine, vp, kl[...]), jnp.where(mine, gp, shift))
+            grad_scores = (probs * grad_weights).astype(jnp.bfloat16)
+            grad_v = jnp.dot(probs.astype(jnp.bfloat16), gh, preferred_element_type=jnp.float32)
+            grad_k = jnp.dot(grad_scores, qh, preferred_element_type=jnp.float32)
+            grad_q = dot_tn(grad_scores, jnp.where(mine, kp, none))
             made.append((grad_q * 0.125, grad_k, grad_v))
         for n in range(3):
             qkv[2 * n + side, rows, cols] = (made[0][n] + made[1][n]).astype(jnp.bfloat16)
-        tick(t + i)
+
+        @pl.when(lax.rem(i, 3) != 2)
+        def _():
+            tick(t + i - (i + 1) // 3)
+
         return carry
 
     lax.fori_loop(0, 8 * pages, pair_backward, 0)
-    t = t + 8 * pages
+    t = t + 8 * pages - 8 * pages // 3
 
     third = [load(12, w_q, buf_c.at[0]), load(13, w_k, buf_d.at[0]), load(14, w_v, buf_e.at[0])]
     third += [load(15 + n, w_other.at[n], ref.at[1]) for n, ref in enumerate((buf_c, buf_d, buf_e))]
@@ -678,7 +754,7 @@
     def weights_loop(i, carry):
         at = b + i
         slot = lax.rem(at, 2)
-        to_twin(at - 2).wait_send()
+        gave_twin(at - 2)
         for r in range(0, full, half):
             made = dot_tn(xb[:, r : r + half], qkv[2 * i]).astype(jnp.bfloat16)
             grads[rows_at(at * BLOCK, BLOCK), r : r + half] = made
@@ -688,13 +764,13 @@
         @pl.when(i >= 1)
         def _():
             take_twin(at - 1)
-
-        to_twin(at).start()
-        tick(t + i)
+            tick(t + i - 1)
+
+        give_twin(at)
         return carry
 
     lax.fori_loop(0, 3, weights_loop, 0)
-    t = t + 3
+    t = t + 2
     b = b + 3
 
     first_core = mp == 0
@@ -709,15 +785,18 @@
         owned.append(jnp.concatenate([bias_in[n : n + 1, :part], bias_in[n + 1 : n + 2, :part]], axis=1))
         others.append(jnp.concatenate([bias_in[n : n + 1, part:], bias_in[n + 1 : n + 2, part:]], axis=1))
     fill = jnp.zeros((QUARTER - len(owned), half), jnp.float32)
-    grads[last_rows : last_rows + QUARTER, :half] = jnp.concatenate(owned + [fill], axis=0).astype(jnp.bfloat16)
-    send_v[...] = jnp.concatenate(others + [fill], axis=0).astype(jnp.bfloat16)
-    vectors = pltpu.make_async_remote_copy(send_v, land_v, vsem, vrsem, device_id=twin, device_id_type=MESH)
-    vectors.start()
+    vec_sum[0] = jnp.concatenate(others + [fill], axis=0)
+    vec_sum[1] = jnp.concatenate(owned + [fill], axis=0)
+
+    def swap_vectors(n):
+        return pltpu.make_async_remote_copy(
+            vec_sum.at[n], vec_land.at[n], vsem.at[n], vrsem.at[n], device_id=swap_peers[n], device_id_type=MESH
+        )
+
+    swap_vectors(0).start()
     take_twin(b - 1)
-    vectors.wait()
-    add_into(grads.at[last_rows : last_rows + QUARTER, :half], land_v)
-    to_twin(b - 2).wait_send()
-    to_twin(b - 1).wait_send()
+    gave_twin(b - 2)
+    gave_twin(b - 1)
     tick(t)
     finish(third)
 
@@ -750,10 +829,22 @@
     lax.fori_loop(0, tiles, end_gifts, 0)
 
     def rest(i, carry):
+        for n in range(5):
+
+            @pl.when(i == t + 2 * n)
+            def _():
+                swap_vectors(n).wait()
+                total = vec_sum[max(n, 1)] + vec_land[n]
+                if n == 4:
+                    vec_out[...] = total
+                else:
+                    vec_sum[n + 1] = total
+                    swap_vectors(n + 1).start()
+
         tick(i)
         return carry
 
-    lax.fori_loop(t, pairs + STAGES[-1], rest, 0)
+    lax.fori_loop(t, last_tick, rest, 0)
     ig_keep.wait()
     ig_send.wait()
 
@@ -775,29 +866,26 @@
     ff_half = w_in.shape[1]
     tiles = ff_half // (BLOCK // 2)
     wide = BLOCK
-    rows = (tiles + 4) * BLOCK + PAIR
+    rows = (tiles + 4) * BLOCK
     f32 = jnp.float32
     bf16 = jnp.bfloat16
     return pl.pallas_call(
         layer_kernel,
         name="layer",
         out_shape=(
-            shape((rows, full)), shape((tokens, half)), shape((tokens, half)), shape((tokens, half)),
-            shape((tokens, half)), shape((tiles, tokens, wide)), shape((tiles, tokens, wide)),
+            shape((rows, full)), shape((QUARTER, half), f32), shape((tokens, half)), shape((tokens, half)),
+            shape((tokens, half)), shape((tokens, half)), shape((tiles, tokens, wide)), shape((tiles, tokens, wide)),
             shape((3, full, half)), shape((half, full)), shape((full, ff_half)), shape((ff_half, full)),
         ),
         in_specs=[HBM] * 8 + [VMEM] * 9 + [SMEM],
-        out_specs=(HBM,) * 11,
+        out_specs=(HBM, VMEM) + (HBM,) * 10,
         scratch_shapes=[
             pltpu.VMEM((rows, full), bf16),
-            pltpu.VMEM((SLOTS, 2, 2 * QUARTER, full), bf16),
-            pltpu.VMEM((SLOTS, 2, 2 * QUARTER, full), bf16),
-            pltpu.VMEM((SLOTS, 2, QUARTER, full), bf16),
-            pltpu.VMEM((SLOTS, 2, QUARTER, full), bf16),
+            *land_shapes(full),
             pltpu.VMEM((2, BLOCK, full), bf16),
             pltpu.VMEM((2, BLOCK, full), bf16),
-            pltpu.VMEM((QUARTER, half), bf16),
-            pltpu.VMEM((QUARTER, half), bf16),
+            pltpu.VMEM((6, QUARTER, half), f32),
+            pltpu.VMEM((5, QUARTER, half), f32),
             pltpu.VMEM((tokens, full), f32),
             pltpu.VMEM((tokens, full), bf16),
             pltpu.VMEM((tokens, full), bf16),
@@ -820,13 +908,13 @@
             pltpu.VMEM((tiles, wide), f32),
             pltpu.VMEM((8, full), f32),
             pltpu.VMEM((seq, 128), bf16),
-            pltpu.SemaphoreType.DMA((7, 2, SLOTS)),
-            pltpu.SemaphoreType.DMA((7, 2, SLOTS)),
-            pltpu.SemaphoreType.DMA((2, SLOTS)),
-            pltpu.SemaphoreType.DMA((2,)),
-            pltpu.SemaphoreType.DMA((2,)),
-            pltpu.SemaphoreType.DMA,
-            pltpu.SemaphoreType.DMA,
+            pltpu.SemaphoreType.DMA((2, sum(SLOTS))),
+            pltpu.SemaphoreType.DMA((2, sum(SLOTS))),
+            pltpu.SemaphoreType.DMA((2, KEEP_SLOTS)),
+            pltpu.SemaphoreType.DMA((2, 2)),
+            pltpu.SemaphoreType.DMA((2, 2)),
+            pltpu.SemaphoreType.DMA((5,)),
+            pltpu.SemaphoreType.DMA((5,)),
             pltpu.SemaphoreType.DMA((2, 6)),
             pltpu.SemaphoreType.DMA((2, 2)),
             pltpu.SemaphoreType.DMA((18,)),
@@ -843,67 +931,78 @@
 
 
 def unpack_kernel(
-    packed, out_mine, out_got, ig_mine, ig_got,
-    output, input_grad, g_q, g_k, g_v, g_o, g_in, g_back,
+    packed, out_mine, out_got, ig_mine, ig_got, vectors,
+    output, input_grad, g_q, g_k, g_v, g_o, g_in, g_back, v_q, v_v, v_o, v_g1, v_s1, v_b, v_g2, v_s2, v_in,
     loaded, wide, passed, isem, osem, csem,
 ):
     mp = lax.axis_index("mp")
     tokens, half = out_mine.shape
     mine = pl.ds(pl.multiple_of(mp * tokens, tokens), tokens)
     other = pl.ds(pl.multiple_of((1 - mp) * tokens, tokens), tokens)
-    pieces = ((out_mine, output.at[mine]), (out_got, output.at[other]), (ig_mine, input_grad.at[mine]), (ig_got, input_grad.at[other]))
+    pieces = (
+        (out_mine, output.at[mine]),
+        (out_got, output.at[other]),
+        (ig_mine, input_grad.at[mine]),
+        (ig_got, input_grad.at[other]),
+    )
     moves = [pltpu.make_async_copy(src, passed.at[i], csem.at[0, i]) for i, (src, _) in enumerate(pieces)]
     leaves = [pltpu.make_async_copy(passed.at[i], dst, csem.at[1, i]) for i, (_, dst) in enumerate(pieces)]
-    for move in moves:
-        move.start()
     part = BLOCK // 2
     full = packed.shape[1]
     tiles = g_back.shape[0] // part
     blocks = tiles + 4
+    slots = wide.shape[0]
 
     def fetch(b):
-        return pltpu.make_async_copy(packed.at[b * BLOCK : (b + 1) * BLOCK], loaded.at[b % 2], isem.at[b % 2])
+        return pltpu.make_async_copy(packed.at[b * BLOCK : (b + 1) * BLOCK], loaded.at[b], isem.at[b])
 
     def stores(b):
-        ref = wide.at[b % 2]
+        ref = wide.at[b % slots]
+        j = tiles - 1 - b
         if b < tiles:
-            pieces = [(ref.at[:part], g_back.at[(tiles - 1 - b) * part : (tiles - b) * part])]
+            pieces = [(ref.at[:part], g_back.at[j * part : (j + 1) * part])]
             for c in range(0, full, part):
-                pieces.append((ref.at[part:, c : c + part], g_in.at[c : c + part, (tiles - 1 - b) * part : (tiles - b) * part]))
+                pieces.append((ref.at[part:, c : c + part], g_in.at[c : c + part, j * part : (j + 1) * part]))
         elif b == tiles:
             pieces = [(ref, g_o)]
         else:
             target = (g_q, g_k, g_v)[b - tiles - 1]
             pieces = [(ref.at[:, :half], target.at[:half]), (ref.at[:, half:], target.at[half:])]
-        return [pltpu.make_async_copy(src, dst, osem.at[b % 2, i]) for i, (src, dst) in enumerate(pieces)]
-
-    fetch(0).start()
-    for move, leave in zip(moves, leaves):
-        move.wait()
-        leave.start()
+        return [pltpu.make_async_copy(src, dst, osem.at[b % slots, i]) for i, (src, dst) in enumerate(pieces)]
+
     for b in range(blocks):
-        if b + 1 < blocks:
-            fetch(b + 1).start()
+        fetch(b).start()
+        if b < len(moves):
+            moves[b].start()
+    for n, ref in enumerate((v_q, v_v, v_o, v_g1, v_s1, v_b, v_g2, v_s2)):
+        ref[...] = vectors[n, :]
+    for n in range(4):
+        v_in[n * half : (n + 1) * half] = vectors[8 + n, :]
+    for b in range(blocks):
         fetch(b).wait()
-        if b >= 2:
-            for store in stores(b - 2):
+        if b >= slots:
+            for store in stores(b - slots):
                 store.wait()
         for r in range(0, BLOCK, CHUNK):
-            wide[b % 2, r : r + CHUNK, :] = loaded[b % 2, r : r + CHUNK, :].astype(jnp.float32)
+            wide[b % slots, r : r + CHUNK, :] = loaded[b, r : r + CHUNK, :].astype(jnp.float32)
         for store in stores(b):
             store.start()
-    for b in (blocks - 2, blocks - 1):
+        if b < len(moves):
+            moves[b].wait()
+            leaves[b].start()
+    for b in range(blocks - slots, blocks):
         for store in stores(b):
             store.wait()
     for leave in leaves:
         leave.wait()
 
 
-def run_unpack(packed, out_mine, out_got, ig_mine, ig_got, tiles):
+def run_unpack(packed, out_mine, out_got, ig_mine, ig_got, vectors, tiles):
     tokens, half = out_mine.shape
     full = 2 * half
     ff_half = tiles * (BLOCK // 2)
     f32 = jnp.float32
+    slots = 6
     return pl.pallas_call(
         unpack_kernel,
         name="unpack",
@@ -911,38 +1010,36 @@
             shape((2 * tokens, half)), shape((2 * tokens, half)),
             shape((full, half), f32), shape((full, half), f32), shape((full, half), f32), shape((half, full), f32),
             shape((full, ff_half), f32), shape((ff_half, full), f32),
+            *[shape((half,), f32)] * 8, shape((ff_half,), f32),
         ),
-        in_specs=[HBM] * 5,
-        out_specs=(HBM,) * 8,
+        in_specs=[HBM] * 5 + [VMEM],
+        out_specs=(HBM,) * 8 + (VMEM,) * 9,
         scratch_shapes=[
-            pltpu.VMEM((2, BLOCK, full), jnp.bfloat16),
-            pltpu.VMEM((2, BLOCK, full), f32),
+            pltpu.VMEM((tiles + 4, BLOCK, full), jnp.bfloat16),
+            pltpu.VMEM((slots, BLOCK, full), f32),
             pltpu.VMEM((4, tokens, half), jnp.bfloat16),
-            pltpu.SemaphoreType.DMA((2,)),
-            pltpu.SemaphoreType.DMA((2, 5)),
+            pltpu.SemaphoreType.DMA((tiles + 4,)),
+            pltpu.SemaphoreType.DMA((slots, 5)),
             pltpu.SemaphoreType.DMA((2, 4)),
         ],
         compiler_params=pltpu.CompilerParams(vmem_limit_bytes=60 << 20),
-        cost_estimate=pl.CostEstimate(flops=0, bytes_accessed=60 << 20, transcendentals=0),
-    )(packed, out_mine, out_got, ig_mine, ig_got)
+    )(packed, out_mine, out_got, ig_mine, ig_got, vectors)
 
 
 def on_core(
     inputs, lengths, w_query, b_query, w_key, w_value, b_value, w_out, b_out, gain_one, shift_one, w_in, b_in, w_back,
     b_back, gain_two, shift_two, cotangent,
 ):
-    half = inputs.shape[1]
     tiles = w_in.shape[1] // (BLOCK // 2)
-    vectors = (b_query, b_value, b_in, b_out, gain_one, shift_one, b_back, gain_two, shift_two)
-    packed, out_mine, out_got, ig_mine, ig_got, *_ = run_layer(
-        inputs, cotangent, w_query, w_key, w_value, w_out, w_in, w_back, vectors, lengths
-    )
-    output, input_grad, g_q, g_k, g_v, g_o, g_in, g_back = run_unpack(packed, out_mine, out_got, ig_mine, ig_got, tiles)
-    at = (tiles + 4) * BLOCK
-    v = packed[at : at + 12, :half].astype(jnp.float32)
+    given = (b_query, b_value, b_in, b_out, gain_one, shift_one, b_back, gain_two, shift_two)
+    packed, vectors, out_mine, out_got, ig_mine, ig_got, *_ = run_layer(
+        inputs, cotangent, w_query, w_key, w_value, w_out, w_in, w_back, given, lengths
+    )
+    output, input_grad, g_q, g_k, g_v, g_o, g_in, g_back, *v = run_unpack(
+        packed, out_mine, out_got, ig_mine, ig_got, vectors, tiles
+    )
     return (
-        output, input_grad, g_q, v[0], g_k, g_v, v[1], g_o, v[2], v[3], v[4], g_in, v[8:12].reshape(-1), g_back, v[5],
-        v[6], v[7],
+        output, input_grad, g_q, v[0], g_k, g_v, v[1], g_o, v[2], v[3], v[4], g_in, v[8], g_back, v[5], v[6], v[7],
     )
 
 

time: 306 us -> 287 us (0.938)
  Pallas kernels: 303 us -> 286 us
    pallas_call x1, Pallas kernels: 287 us -> 270 us  [run_layer(): pl.pallas_call(layer_kernel, name='layer', out_shape=(shape((rows, full))...]
where the time goes in v1:
time: 287 us
  Pallas kernels  286 us (100%)
    pallas_call x1, Pallas kernels, run_layer(): pl.pallas_call(layer_kernel, name='layer', out_shape=(shape((rows, full))...  270 us
    pallas_call x1, Pallas kernels, run_unpack(): pl.pallas_call(unpack_kernel, name='unpack', out_shape=(shape((2 * tokens...  16.5 us

profile of v1, /device:TPU:0, one launch (start us, length us, event | category | flops | bytes accessed | tf_op | source)
XLA Modules:
  0.0 287.1 jit_solution(12400547386145457775)
XLA Ops:
  0.7 269.8 %layer.1 = (bf16[6144,1024]{1,0:T(8,128)(2,1)}, f32[16,512]{1,0:T(8,128)}, bf16[1024,512]{1,0:T(8,128)(2,1)}, bf16[1024,512]{1,0:T(8,128)(2,1)}, bf16[1024,512]{...) custom-call(bf16[2048,512]{1,0:T(8,128)(2,1)} %inputs.1, ...), custom_call_target="tpu_custom_call" | custom-call | tf_op jit(solution)/shard_map/layer/pallas_call | solution.py:872
  270.5 16.5 %unpack.1 = (bf16[2048,512]{1,0:T(8,128)(2,1)}, bf16[2048,512]{1,0:T(8,128)(2,1)}, f32[1024,512]{1,0:T(8,128)}, f32[1024,512]{1,0:T(8,128)}, f32[1024,512]{1,0:T...) custom-call(bf16[6144,1024]{1,0:T(8,128)(2,1)} %get-tuple-element.40, ...), custom_call_target="tpu_custom_call" | custom-call | tf_op jit(solution)/shard_map/unpack/pallas_call | solution.py:1006

commit v2 on v1

--- a/solution.py
+++ b/solution.py
@@ -406,36 +406,37 @@
     q_one = jnp.where(lane % 64 == 3, 1.0, 0.0).astype(jnp.bfloat16)
 
     def pair_forward(i, carry):
-        page, pair = i // 8, lax.rem(i, 8)
-
-        @pl.when(pair == 0)
+        page, first_pair = i // 2, 4 * lax.rem(i, 2)
+
+        @pl.when(first_pair == 0)
         def _():
             kl[...] = key_lanes(lens[mp * pages + page], seq)
 
         rows = pl.ds(pl.multiple_of(page * seq, seq), seq)
-        side = pair // 4
-        cols = pl.ds(pl.multiple_of(lax.rem(pair, 4) * 128, 128), 128)
-        kp = qkv[2 + side, rows, cols]
-        vp = qkv[4 + side, rows, cols]
-        qp = qkv[side, rows, cols] * jnp.bfloat16(0.125)
-        one = jnp.ones_like(vp)
-        outs = []
-        for h in (0, 1):
-            mine = low_lanes if h == 0 else jnp.logical_not(low_lanes)
-            scores = dot_nt(jnp.where(mine, qp, q_one), jnp.where(mine, kp, kl[...]))
-            top = jnp.max(scores, axis=1, keepdims=True)
-            weights = jnp.exp(scores - top).astype(jnp.bfloat16)
-            outs.append((top, jnp.dot(weights, jnp.where(mine, vp, one), preferred_element_type=jnp.float32)))
-        (top0, out0), (top1, out1) = outs
-        total = jnp.where(low_lanes, out1, out0)
-        value = jnp.where(low_lanes, out0, out1) / pltpu.roll(total, 64, 1)
-        neg = -(jnp.where(low_lanes, top1, top0) + jnp.log(total))
-        mixed = spread_lanes(neg, lane, q_one)
-        ctx[side, rows, cols] = value.astype(jnp.bfloat16)
-        aux[side, rows, cols] = mixed
+        for pair in [first_pair + n for n in range(4)]:
+            side = pair // 4
+            cols = pl.ds(pl.multiple_of(lax.rem(pair, 4) * 128, 128), 128)
+            kp = qkv[2 + side, rows, cols]
+            vp = qkv[4 + side, rows, cols]
+            qp = qkv[side, rows, cols] * jnp.bfloat16(0.125)
+            one = jnp.ones_like(vp)
+            outs = []
+            for h in (0, 1):
+                mine = low_lanes if h == 0 else jnp.logical_not(low_lanes)
+                scores = dot_nt(jnp.where(mine, qp, q_one), jnp.where(mine, kp, kl[...]))
+                top = jnp.max(scores, axis=1, keepdims=True)
+                weights = jnp.exp(scores - top).astype(jnp.bfloat16)
+                outs.append((top, jnp.dot(weights, jnp.where(mine, vp, one), preferred_element_type=jnp.float32)))
+            (top0, out0), (top1, out1) = outs
+            total = jnp.where(low_lanes, out1, out0)
+            value = jnp.where(low_lanes, out0, out1) / pltpu.roll(total, 64, 1)
+            neg = -(jnp.where(low_lanes, top1, top0) + jnp.log(total))
+            mixed = spread_lanes(neg, lane, q_one)
+            ctx[side, rows, cols] = value.astype(jnp.bfloat16)
+            aux[side, rows, cols] = mixed
         return carry
 
-    lax.fori_loop(0, 8 * pages, pair_forward, 0)
+    lax.fori_loop(0, 2 * pages, pair_forward, 0)
 
     def fetch_in(j, slot):
         at = pl.ds(pl.multiple_of(j * part, part), part)
@@ -471,7 +472,7 @@
 
     got_gifts(0)
     start(fetch_in(0, 0))
-    step = 256
+    step = 512
 
     def norm_one(i, carry):
         rows = pl.ds(pl.multiple_of(i * step, step), step)
@@ -629,15 +630,11 @@
         @pl.when(b >= 1)
         def _():
             take_half(b - 1, 1)
-            tick(3 * b - 2)
+            tick(3 * b - 1)
 
         acc[...] += dot_nt(inner_g[...], buf_e[slot])
         take_half(b, 0)
-
-        @pl.when(b >= 1)
-        def _():
-            tick(3 * b - 1)
-
+        tick(3 * b)
         for c in range(0, full, part):
             made = dot_tn(low[:, c : c + part], inner_g[...]).astype(jnp.bfloat16)
             grads[rows_at(base + part, part), c : c + part] = made[:, :part]
@@ -653,11 +650,11 @@
         def _():
             start(fetch_made(j - 2, slot) + fetch_in(j - 2, slot) + fetch_back(j - 2, slot))
 
-        tick(3 * b)
+        tick(3 * b + 1)
         return carry
 
     lax.fori_loop(0, tiles, backward_tile, 0)
-    t = 3 * tiles - 2
+    t = 3 * tiles - 1
 
     second = [load(10, w_o, buf_f.at[0]), load(11, w_oo, buf_f.at[1])]
     start(second)
@@ -704,47 +701,50 @@
     t = t + 3
 
     def pair_backward(i, carry):
-        page, pair = i // 8, lax.rem(i, 8)
-
-        @pl.when(pair == 0)
+        page, first_pair = i // 4, 2 * lax.rem(i, 4)
+
+        @pl.when(first_pair == 0)
         def _():
             kl[...] = key_lanes(lens[mp * pages + page], seq)
 
-        side = pair // 4
-        rows = pl.ds(pl.multiple_of(page * seq, seq), seq)
-        cols = pl.ds(pl.multiple_of(lax.rem(pair, 4) * 128, 128), 128)
-        qp = qkv[side, rows, cols] * jnp.bfloat16(0.125)
-        kp = qkv[2 + side, rows, cols]
-        vp = qkv[4 + side, rows, cols]
-        extra = aux[side, rows, cols]
-        gp = buf_e[side, rows, cols]
-        cp = ctx[side, rows, cols]
-        none = jnp.zeros_like(gp)
-        product = gp.astype(jnp.float32) * cp.astype(jnp.float32)
-        sums = [jnp.sum(jnp.where(mine, product, 0.0), axis=1, keepdims=True) for mine in (low_lanes, high_lanes)]
-        shift = spread_lanes(-jnp.where(low_lanes, sums[1], sums[0]), lane, none)
-        made = []
-        for mine in (low_lanes, high_lanes):
-            qh = jnp.where(mine, qp, none)
-            gh = jnp.where(mine, gp, none)
-            probs = jnp.exp(dot_nt(jnp.where(mine, kp, kl[...]), jnp.where(mine, qp, extra)))
-            grad_weights = dot_nt(jnp.where(mine, vp, kl[...]), jnp.where(mine, gp, shift))
-            grad_scores = (probs * grad_weights).astype(jnp.bfloat16)
-            grad_v = jnp.dot(probs.astype(jnp.bfloat16), gh, preferred_element_type=jnp.float32)
-            grad_k = jnp.dot(grad_scores, qh, preferred_element_type=jnp.float32)
-            grad_q = dot_tn(grad_scores, jnp.where(mine, kp, none))
-            made.append((grad_q * 0.125, grad_k, grad_v))
-        for n in range(3):
-            qkv[2 * n + side, rows, cols] = (made[0][n] + made[1][n]).astype(jnp.bfloat16)
-
-        @pl.when(lax.rem(i, 3) != 2)
-        def _():
-            tick(t + i - (i + 1) // 3)
+        for pair in (first_pair, first_pair + 1):
+            side = pair // 4
+            rows = pl.ds(pl.multiple_of(page * seq, seq), seq)
+            cols = pl.ds(pl.multiple_of(lax.rem(pair, 4) * 128, 128), 128)
+            qp = qkv[side, rows, cols] * jnp.bfloat16(0.125)
+            kp = qkv[2 + side, rows, cols]
+            vp = qkv[4 + side, rows, cols]
+            extra = aux[side, rows, cols]
+            gp = buf_e[side, rows, cols]
+            cp = ctx[side, rows, cols]
+            none = jnp.zeros_like(gp)
+            product = gp.astype(jnp.float32) * cp.astype(jnp.float32)
+            sums = [jnp.sum(jnp.where(mine, product, 0.0), axis=1, keepdims=True) for mine in (low_lanes, high_lanes)]
+            shift = spread_lanes(-jnp.where(low_lanes, sums[1], sums[0]), lane, none)
+            made = []
+            for mine in (low_lanes, high_lanes):
+                qh = jnp.where(mine, qp, none)
+                gh = jnp.where(mine, gp, none)
+                probs = jnp.exp(dot_nt(jnp.where(mine, kp, kl[...]), jnp.where(mine, qp, extra)))
+                grad_weights = dot_nt(jnp.where(mine, vp, kl[...]), jnp.where(mine, gp, shift))
+                grad_scores = (probs * grad_weights).astype(jnp.bfloat16)
+                grad_v = jnp.dot(probs.astype(jnp.bfloat16), gh, preferred_element_type=jnp.float32)
+                grad_k = jnp.dot(grad_scores, qh, preferred_element_type=jnp.float32)
+                grad_q = dot_tn(grad_scores, jnp.where(mine, kp, none))
+                made.append((grad_q * 0.125, grad_k, grad_v))
+            for n in range(3):
+                qkv[2 * n + side, rows, cols] = (made[0][n] + made[1][n]).astype(jnp.bfloat16)
+
+        tick(t + i + i // 4)
+
+        @pl.when(lax.rem(i, 4) == 3)
+        def _():
+            tick(t + i + 1 + i // 4)
 
         return carry
 
-    lax.fori_loop(0, 8 * pages, pair_backward, 0)
-    t = t + 8 * pages - 8 * pages // 3
+    lax.fori_loop(0, 4 * pages, pair_backward, 0)
+    t = t + 10
 
     third = [load(12, w_q, buf_c.at[0]), load(13, w_k, buf_d.at[0]), load(14, w_v, buf_e.at[0])]
     third += [load(15 + n, w_other.at[n], ref.at[1]) for n, ref in enumerate((buf_c, buf_d, buf_e))]

time: 287 us -> 286 us (level); the launches traced: 287 us -> 283 us
  Pallas kernels: 286 us -> 282 us
    pallas_call x1, Pallas kernels: 270 us -> 265 us  [run_layer(): pl.pallas_call(layer_kernel, name='layer', out_shape=(shape((rows, full))...]
where the time goes in v2:
time: 286 us; the launch traced here: 283 us
  Pallas kernels  282 us (99%)
    pallas_call x1, Pallas kernels, run_layer(): pl.pallas_call(layer_kernel, name='layer', out_shape=(shape((rows, full))...  265 us
    pallas_call x1, Pallas kernels, run_unpack(): pl.pallas_call(unpack_kernel, name='unpack', out_shape=(shape((2 * tokens...  16.5 us

profile of v2, /device:TPU:0, one launch (start us, length us, event | category | flops | bytes accessed | tf_op | source)
XLA Modules:
  0.0 282.5 jit_solution(12309340400108080324)
XLA Ops:
  0.7 265.1 %layer.1 = (bf16[6144,1024]{1,0:T(8,128)(2,1)}, f32[16,512]{1,0:T(8,128)}, bf16[1024,512]{1,0:T(8,128)(2,1)}, bf16[1024,512]{1,0:T(8,128)(2,1)}, bf16[1024,512]{...) custom-call(bf16[2048,512]{1,0:T(8,128)(2,1)} %inputs.1, ...), custom_call_target="tpu_custom_call" | custom-call | tf_op jit(solution)/shard_map/layer/pallas_call | solution.py:872
  265.8 16.5 %unpack.1 = (bf16[2048,512]{1,0:T(8,128)(2,1)}, bf16[2048,512]{1,0:T(8,128)(2,1)}, f32[1024,512]{1,0:T(8,128)}, f32[1024,512]{1,0:T(8,128)}, f32[1024,512]{1,0:T...) custom-call(bf16[6144,1024]{1,0:T(8,128)(2,1)} %get-tuple-element.40, ...), custom_call_target="tpu_custom_call" | custom-call | tf_op jit(solution)/shard_map/unpack/pallas_call | solution.py:1006
